TPU v7x, 256 devices: a whole 4x4x8 slice. The times are simulated.
256 devices in a mesh: lat: 16 (over y, x_lo, core), lon: 16 (over x_hi, z).
Axes of the slice: x: 4 (x_hi: 2, x_lo: 2; x = x_hi * 2 + x_lo), y: 4, z: 8, core: 2. Of those that a mesh axis runs over, the one named last changes fastest.
Arguments:
- state: bfloat16 [256, 384, 2048], P(None, 'lat', 'lon'), may hold values from -6 to 6
- obs_values: bfloat16 [64, 524288], P(None, ('lat', 'lon')), may hold values from -6 to 6
- obs_offsets: float32 [2, 524288], P(None, ('lat', 'lon')), may hold values from 0 to 1
- obs_cell: int32 [524288], P(('lat', 'lon')), may hold values from 0 to 3071, as said below
- obs_count: int32 [256], P(('lat', 'lon')), may hold values from 64 to 2048, as said below
- w_in: bfloat16 [65, 256], replicated, may hold values from -0.75 to 0.75
- dw_weight: float32 [256, 7, 7], replicated, may hold values from -0.875 to 0.875
- dw_bias: float32 [256], replicated, may hold values from -3 to 3
- norm_gain: float32 [256], replicated, may hold values from 0.1 to 1.9
- norm_bias: float32 [256], replicated, may hold values from -3 to 3
- w_up: bfloat16 [256, 1024], replicated, may hold values from -0.375 to 0.375
- up_bias: float32 [1024], replicated, may hold values from -3 to 3
- w_down: bfloat16 [1024, 256], replicated, may hold values from -0.1875 to 0.1875
- down_bias: float32 [256], replicated, may hold values from -3 to 3
- layer_scale: float32 [256], replicated, may hold values from 0.1 to 1.9
Outputs:
- result: bfloat16 [256, 384, 2048], P(None, 'lat', 'lon')
Inputs may be any that keep to these rules, and one draw needn't show every extreme that they name: obs_cell numbers a cell inside the slot's own tile as row * 128 + column, row below 24 and column below 128, padding slots included; tiles are numbered along latitude first, then longitude, tile t holding latitude rows from 24 * (t // 16) and longitude columns from 128 * (t % 16). The live slots of each tile are its first obs_count slots; the rest are padding.
All inputs are finite; a program needn't handle non-finite values.
Results may differ from a plain program's by a relative error of at most 0.0065.
Values may be sent and summed in bfloat16 or wider, within the bound.
No kernel may reach another device: no remote copies, remote signals or barrier semaphores. Data moves between devices by JAX's collectives and lax.ppermute only.
A program may use at most 128 MiB of HBM per device.

v0:
```python
import jax
import jax.numpy as jnp
from jax import lax
from jax.experimental import pallas as pl
from jax.experimental.pallas import tpu as pltpu
from jax.sharding import PartitionSpec as P

W = 4
SRC = 80
ROWS = 32
OBS_BLOCK = 512
GRID_ROWS = 384
CB = 64
RB = 8
BF = jnp.bfloat16
F = jnp.float32
MIB = 2**20
LAT_STATE = 9 * SRC
LAT_MSG = 9 * SRC + 3 * 256
LON_STATE = 2 * SRC
LON_MSG = 2 * SRC + 256
RIMS = 2 * SRC + 2 * 256

inverse_width = 1.0 / (2.0 * 1.5 * 1.5)


def lanes(rows):
    return lax.broadcasted_iota(jnp.int32, (rows, 128), 1)


def sums_kernel(count, row_base, vals_in, offs_in, cell_in, state_in, sums, up, down, vals, offs, cell, state, scaled, acc, sems):
    live_count = count[0]
    copies = [
        pltpu.make_async_copy(vals_in, vals, sems.at[0]),
        pltpu.make_async_copy(offs_in, offs, sems.at[1]),
        pltpu.make_async_copy(cell_in, cell, sems.at[2]),
        pltpu.make_async_copy(state_in.at[:, 0:8, :], state.at[:, 0:8, :], sems.at[3]),
        pltpu.make_async_copy(state_in.at[:, 16:24, :], state.at[:, 8:16, :], sems.at[4]),
    ]
    for copy in copies:
        copy.start()
    acc[...] = jnp.zeros(acc.shape, F)
    for copy in copies[:3]:
        copy.wait()

    def add_block(b, _):
        k0 = pl.multiple_of(b * OBS_BLOCK, OBS_BLOCK)
        ks = pl.ds(k0, OBS_BLOCK)
        where_cell = cell[:, ks]
        row = where_cell >> 7
        col = where_cell & 127
        slot = lax.broadcasted_iota(jnp.int32, (1, OBS_BLOCK), 1) + k0
        row = jnp.where(slot < live_count, row, -100)

        def weight(offset, place, centre, valid):
            apart = place - centre
            spread = offset - apart.astype(F) - 0.5
            inside = (jnp.abs(apart) <= W) & valid
            return jnp.where(inside, jnp.exp(-spread * spread * inverse_width), 0.0)

        place = lax.broadcasted_iota(jnp.int32, (ROWS, OBS_BLOCK), 0) - W
        on_grid = (place + row_base[0] >= 0) & (place + row_base[0] < GRID_ROWS)
        lat_weight = weight(offs[0:1, ks], place, row, on_grid)
        place = lax.broadcasted_iota(jnp.int32, (136, OBS_BLOCK), 0)
        first = weight(offs[1:2, ks], place, col, place < 128 + W)
        place = lax.broadcasted_iota(jnp.int32, (8, OBS_BLOCK), 0) - 8
        last = weight(offs[1:2, ks], place, col, place >= -W)
        lon_weight = jnp.concatenate([first, jnp.zeros((112, OBS_BLOCK), F), last], 0).astype(BF)
        ones = jnp.where(lax.broadcasted_iota(jnp.int32, (SRC - 64, OBS_BLOCK), 0) == 0, 1.0, 0.0)
        v = jnp.concatenate([vals[:, ks].astype(F), ones], 0)
        for p in range(ROWS):
            scaled[p * SRC:(p + 1) * SRC] = (v * lat_weight[p:p + 1]).astype(BF)
        for m in range(0, ROWS * SRC, 640):
            acc[m:m + 640] += lax.dot_general(
                scaled[m:m + 640], lon_weight, (((1,), (1,)), ((), ())), preferred_element_type=F)
        return 0

    lax.fori_loop(0, (live_count + OBS_BLOCK - 1) // OBS_BLOCK, add_block, 0)
    for copy in copies[3:]:
        copy.wait()
    for p in range(ROWS):
        sums[p] = acc[p * SRC:(p + 1) * SRC].astype(BF)
    for msg, first, state_tile, state_row in ((up, 0, 0, 0), (down, 24, 8, 5)):
        side = jnp.zeros((SRC, 128), F)
        for i in range(8):
            part = acc[(first + i) * SRC:(first + i + 1) * SRC]
            msg[i * SRC:(i + 1) * SRC] = part[:, :128].astype(BF)
            moved = pltpu.roll(part[:, 128:], i * 8 + 4, 1)
            side = jnp.where((lanes(SRC) >> 3) == i, moved, side)
        msg[8 * SRC:9 * SRC] = side.astype(BF)
        for c in range(0, 256, 16):
            x = jnp.swapaxes(state[c:c + 16, state_tile:state_tile + 8, :].astype(F), 0, 1).astype(BF)
            for j in range(3):
                msg[LAT_STATE + j * 256 + c:LAT_STATE + j * 256 + c + 16] = x[state_row + j]


def observation_sums(obs_values, obs_offsets, obs_cell, obs_count, row_base, state):
    S = pl.BlockSpec(memory_space=pltpu.SMEM)
    V = pl.BlockSpec(memory_space=pltpu.VMEM)
    shape = jax.ShapeDtypeStruct
    return pl.pallas_call(
        sums_kernel, name="observation_sums",
        out_shape=(shape((ROWS, SRC, 256), BF), shape((LAT_MSG, 128), BF), shape((LAT_MSG, 128), BF)),
        in_specs=[S, S] + [pl.BlockSpec(memory_space=pl.ANY)] * 4, out_specs=(V,) * 3,
        scratch_shapes=[
            pltpu.VMEM((64, 2048), BF), pltpu.VMEM((2, 2048), F), pltpu.VMEM((1, 2048), jnp.int32), pltpu.VMEM((256, 16, 128), BF),
            pltpu.VMEM((ROWS * SRC, OBS_BLOCK), BF), pltpu.VMEM((ROWS * SRC, 256), F), pltpu.SemaphoreType.DMA((5,)),
        ],
        compiler_params=pltpu.CompilerParams(vmem_limit_bytes=56 * MIB),
    )(obs_count, row_base, obs_values, obs_offsets, obs_cell.reshape(1, -1), state)


def place(p):
    return 15 - p % 16


def pack(packed, p, main, side):
    lane = lanes(SRC)
    k, shift = p // 16, place(p) * 8 + 4
    here = (lane >> 3) == place(p)
    packed[0][k] = jnp.where(here, pltpu.roll(jnp.where(lane < 4, main, side), shift, 1), packed[0][k])
    packed[1][k] = jnp.where(here, pltpu.roll(jnp.where(lane >= 124, main, side), shift, 1), packed[1][k])


def rows_kernel(state, sums, rows, rims):
    def turn(i, _):
        c0 = pl.multiple_of(i * 16, 16)
        rows[:, pl.ds(c0, 16), :] = jnp.swapaxes(state[pl.ds(c0, 16)].astype(F), 0, 1).astype(BF)
        return 0

    lax.fori_loop(0, 16, turn, 0)
    for c in range(0, 256, 64):
        packed = [jnp.zeros((64, 128), F) for _ in range(2)]
        for r in range(24):
            p = r + W
            moved = pltpu.roll(rows[r, c:c + 64, :].astype(F), place(p) * 8 + 4, 1)
            packed[p // 16] = jnp.where((lanes(64) >> 3) == place(p), moved, packed[p // 16])
        for k in range(2):
            rims[LON_STATE + k * 256 + c:LON_STATE + k * 256 + c + 64] = packed[k].astype(BF)
    packed = [[jnp.zeros((SRC, 128), F) for _ in range(2)] for _ in range(2)]
    for p in range(8, 24):
        pack(packed, p, sums[p, :, :128].astype(F), sums[p, :, 128:].astype(F))
    for k in range(2):
        rims[k * SRC:(k + 1) * SRC] = packed[0][k].astype(BF)
        rims[RIMS + k * SRC:RIMS + (k + 1) * SRC] = packed[1][k].astype(BF)


def state_rows(state, sums):
    shape = jax.ShapeDtypeStruct
    return pl.pallas_call(
        rows_kernel, name="state_rows", out_shape=(shape((24, 256, 128), BF), shape((RIMS + LON_STATE, 128), BF)),
        cost_estimate=pl.CostEstimate(flops=10**7, bytes_accessed=8 * 10**6, transcendentals=0),
        compiler_params=pltpu.CompilerParams(vmem_limit_bytes=16 * MIB),
    )(state, sums)


def edge_kernel(sums, rims, above, below, edge, left, right):
    lane = lanes(SRC)
    outer = (lane < 4) | (lane >= 124)
    packed = [[rims[first + k * SRC:first + (k + 1) * SRC].astype(F) for k in range(2)] for first in (0, RIMS)]
    for e in range(16):
        p = e if e < 8 else e + 16
        msg, i = (above, p) if p < 8 else (below, p - 24)
        moved = pltpu.roll(msg[8 * SRC:9 * SRC].astype(F), 124 - i * 8, 1)
        main = sums[p, :, :128].astype(F) + msg[i * SRC:(i + 1) * SRC].astype(F)
        side = sums[p, :, 128:].astype(F) + jnp.where(outer, moved, 0.0)
        edge[e] = main.astype(BF)
        pack(packed, p, main, side)
    for k in range(2):
        left[k * SRC:(k + 1) * SRC] = packed[0][k].astype(BF)
        right[k * SRC:(k + 1) * SRC] = packed[1][k].astype(BF)
    early = (lanes(64) & 7) < 4
    for c in range(0, 256, 64):
        halves = []
        for k, msg, first in ((0, above, 1), (1, below, 28)):
            at = LON_STATE + k * 256 + c
            out = rims[at:at + 64].astype(F)
            for j in range(3):
                p = first + j
                x = msg[LAT_STATE + j * 256 + c:LAT_STATE + j * 256 + c + 64].astype(F)
                out = jnp.where((lanes(64) >> 3) == place(p), pltpu.roll(x, place(p) * 8 + 4, 1), out)
            halves.append(out)
        at = slice(LON_STATE + c, LON_STATE + c + 64)
        left[at] = jnp.where(early, pltpu.roll(halves[1], 124, 1), halves[0]).astype(BF)
        right[at] = jnp.where(early, halves[0], pltpu.roll(halves[1], 4, 1)).astype(BF)


def edge_sums(sums, rims, above, below):
    shape = jax.ShapeDtypeStruct
    return pl.pallas_call(
        edge_kernel, name="edge_sums",
        out_shape=(shape((16, SRC, 128), BF), shape((LON_MSG, 128), BF), shape((LON_MSG, 128), BF)),
        compiler_params=pltpu.CompilerParams(vmem_limit_bytes=16 * MIB),
    )(sums, rims, above, below)


def prepare_kernel(taps, w_in, w_up, w_down, b1, toe, wi, w1, w2, b1c, smat, padded, base):
    smat[...] = shift_matrix()
    padded[...] = jnp.zeros(padded.shape, F)
    padded[0:65] = w_in[...].astype(F)
    wi[...] = padded[...].T.astype(BF)
    w1[...] = w_up[...].T
    w2[...] = w_down[...].T
    b1c[...] = b1[...].T
    base[...] = jnp.zeros(base.shape, F)
    for v in range(7):
        for u in range(7):
            base[32 * v + 1 + u:32 * v + 2 + u] = taps[u, v:v + 1]
    base[...] = base[...].T

    def step(i, _):
        rows = base[pl.ds(pl.multiple_of(i * 8, 8), 8), :]
        for k in range(8):
            parts = []
            for ln in range(2):
                b = jnp.broadcast_to(rows[k:k + 1, ln * 128:(ln + 1) * 128], (24, 128))
                parts.append(pltpu.roll(b, 0, 1, stride=1, stride_axis=0))
            y = jnp.concatenate(parts, 1).astype(BF)
            toe[i * 4 + k // 2, (k % 2) * 24:(k % 2) * 24 + 24, :] = y[:, :224]
        return 0

    lax.fori_loop(0, 32, step, 0)


def prepare(dw_weight, w_in, w_up, w_down, up_bias):
    shape = jax.ShapeDtypeStruct
    return pl.pallas_call(
        prepare_kernel, name="prepare",
        out_shape=(shape((128, 48, 224), BF), shape((256, SRC), BF), shape((1024, 256), BF), shape((256, 1024), BF), shape((128, 8), F), shape((256, 768), BF)),
        scratch_shapes=[pltpu.VMEM((SRC, 256), F), pltpu.VMEM((256, 256), F)],
        cost_estimate=pl.CostEstimate(flops=10**7, bytes_accessed=8 * 10**6, transcendentals=0),
        compiler_params=pltpu.CompilerParams(vmem_limit_bytes=16 * MIB),
    )(jnp.transpose(dw_weight, (1, 2, 0)), w_in, w_up, w_down, up_bias.reshape(8, 128))


def shift_matrix():
    lane = lax.broadcasted_iota(jnp.int32, (256, 768), 0)
    out = lax.broadcasted_iota(jnp.int32, (256, 768), 1)
    j = lane & 7
    col = jnp.where(lane < 128, lane, jnp.where(j < 4, j - 4, j + 124))
    k = out // 128
    d = jnp.where(k < 3, k - 3, k - 2)
    return jnp.where(col == out % 128 + d, 1.0, 0.0).astype(BF)


def encode_kernel(sums, edge, above, below, rows, wi, native, mixed):
    def encode(*cases):
        both = jnp.dot(wi[...], jnp.concatenate([main for _, main, _ in cases], 1), preferred_element_type=F)
        for n, (p, _, state) in enumerate(cases):
            mixed[p] = (both[:, n * 128:(n + 1) * 128] + state.astype(F)).astype(BF)

    mixed[0] = jnp.zeros((256, 128), BF)
    mixed[31] = jnp.zeros((256, 128), BF)
    for j in range(3):
        at = slice(LAT_STATE + j * 256, LAT_STATE + j * 256 + 256)
        encode((1 + j, edge[1 + j], above[at]), (28 + j, edge[12 + j], below[at]))

    def edge_row(j, _):
        encode((4 + j, edge[4 + j], rows[j]), (24 + j, edge[8 + j], rows[20 + j]))
        return 0

    def inner_row(j, _):
        encode((8 + j, sums[8 + j, :, :128], rows[4 + j]), (16 + j, sums[16 + j, :, :128], rows[12 + j]))
        return 0

    lax.fori_loop(0, 4, edge_row, 0)
    lax.fori_loop(0, 8, inner_row, 0)

    def turn(i, _):
        c0 = pl.multiple_of(i * CB, CB)
        native[pl.ds(c0, CB)] = jnp.swapaxes(mixed[:, pl.ds(c0, CB), :].astype(F), 0, 1).astype(BF)
        return 0

    lax.fori_loop(0, 256 // CB, turn, 0)


def encode(*arrays):
    return pl.pallas_call(
        encode_kernel, name="encode", out_shape=jax.ShapeDtypeStruct((256, ROWS, 128), BF),
        scratch_shapes=[pltpu.VMEM((ROWS, 256, 128), BF)],
        cost_estimate=pl.CostEstimate(flops=10**8, bytes_accessed=8 * 10**6, transcendentals=0),
        compiler_params=pltpu.CompilerParams(vmem_limit_bytes=20 * MIB),
    )(*arrays)


def block_kernel(dwb, gain, nbias, db, ls, partial, left, right, from_left, from_right,
                 toe, wi, w1, b1, w2, smat, out, native, sides, inward, mext, xs, filt, xbuf, obuf, result, sems):
    first = (lanes(SRC) & 7) < 4
    parts = []
    for k in range(2):
        at = slice(k * SRC, (k + 1) * SRC)
        a, b = from_left[at].astype(F), from_right[at].astype(F)
        parts.append(jnp.where(first, left[at].astype(F) + a, right[at].astype(F) + b))
        parts.append(jnp.where(first, b, a))
    both = jnp.dot(wi[...], jnp.concatenate(parts, 1).astype(BF), preferred_element_type=F)
    first = (lanes(256) & 7) < 4
    a, b = from_left[LON_STATE:LON_STATE + 256].astype(F), from_right[LON_STATE:LON_STATE + 256].astype(F)
    rims = (jnp.where(first, a, b), jnp.where(first, pltpu.roll(a, 124, 1), pltpu.roll(b, 4, 1)))
    for k in range(2):
        sides[:, k * 128:(k + 1) * 128] = (both[:, 2 * k * 128:(2 * k + 1) * 128] + rims[k]).astype(BF).astype(F)
        inward[:, k * 128:(k + 1) * 128] = both[:, (2 * k + 1) * 128:(2 * k + 2) * 128]
    slot = (lanes(16) >> 3) == 15 - lax.broadcasted_iota(jnp.int32, (16, 128), 0)
    outer = (lanes(16) < 4) | (lanes(16) >= 124)

    def filt_step(i, carry):
        pivot, s1, s2 = carry
        c0 = pl.multiple_of(i * CB, CB)
        side, more = sides[pl.ds(c0, CB)], inward[pl.ds(c0, CB)]
        for c in range(CB):
            for k in range(2):
                at = slice(c * 32 + k * 16, c * 32 + k * 16 + 16)
                ks = slice(k * 128, (k + 1) * 128)
                spread = jnp.broadcast_to(side[c:c + 1, ks], (16, 128))
                mext[at, 128:] = jnp.where(slot, spread, 0.0).astype(BF)
                moved = pltpu.roll(jnp.broadcast_to(more[c:c + 1, ks], (16, 128)), 4, 1, stride=8, stride_axis=0)
                main = (partial[c0 + c, k * 16:k * 16 + 16].astype(F) + jnp.where(outer, moved, 0.0)).astype(BF)
                mext[at, :128] = main
                native[c0 + c, k * 16:k * 16 + 16] = main
                xs[c // 2, 96 + k * 16:112 + k * 16, (c % 2) * 128:(c % 2) * 128 + 128] = main
        for j in range(3):
            z = jnp.dot(mext[...], smat[:, j * 256:(j + 1) * 256], preferred_element_type=F).astype(BF)
            for half in range(2):
                k = 2 * j + half
                v = k if k < 3 else k + 1
                zz = z[:, half * 128:(half + 1) * 128]
                for c in range(CB):
                    xs[c // 2, v * 32:(v + 1) * 32, (c % 2) * 128:(c % 2) * 128 + 128] = zz[c * 32:(c + 1) * 32]
        for k in range(CB // 2):
            o = jnp.dot(toe[i * (CB // 2) + k], xs[k], preferred_element_type=F)
            for c, y in ((c0 + 2 * k, o[:24, :128]), (c0 + 2 * k + 1, o[24:, 128:])):
                y = y + dwb[c]
                if k == 0:
                    pivot = jnp.where(c == 0, y, pivot)
                y = y - pivot
                filt[c] = y
                s1 = s1 + y
                s2 = s2 + y * y
        return pivot, s1, s2

    zero = jnp.zeros((24, 128), F)
    _, s1, s2 = lax.fori_loop(0, 256 // CB, filt_step, (zero, zero, zero))
    mean = s1 * (1.0 / 256)
    rstd = lax.rsqrt(jnp.maximum(s2 * (1.0 / 256) - mean * mean, 0.0) + 1e-6)

    def norm_step(i, _):
        c0 = pl.multiple_of(i * 16, 16)
        ys = [((filt[c0 + k] - mean) * rstd) * gain[c0 + k] + nbias[c0 + k] for k in range(16)]
        xbuf[:, pl.ds(c0, 16), :] = jnp.swapaxes(jnp.stack(ys, 0), 0, 1).astype(BF)
        return 0

    lax.fori_loop(0, 16, norm_step, 0)

    def mlp_step(i, _):
        x = jnp.concatenate([xbuf[i * RB + k] for k in range(RB)], 1)
        h = jnp.dot(w1[...], x, preferred_element_type=F)
        gs = []
        for k in range(8):
            hk = h[k * 128:(k + 1) * 128] + b1[:, k:k + 1]
            gs.append(((0.5 * hk) * (1.0 + lax.erf(hk * 0.7071067811865476))).astype(BF))
        o = jnp.dot(w2[...], jnp.concatenate(gs, 0), preferred_element_type=F)
        for k in range(RB):
            obuf[i * RB + k] = o[:, k * 128:(k + 1) * 128]
        return 0

    lax.fori_loop(0, 24 // RB, mlp_step, 0)

    def out_step(i, _):
        c0 = pl.multiple_of(i * 16, 16)
        o = jnp.swapaxes(obuf[:, pl.ds(c0, 16), :], 0, 1)
        m = native[pl.ds(c0, 16)].astype(F)
        for k in range(16):
            result[c0 + k] = (m[k, 4:28] + (o[k] + db[c0 + k]) * ls[c0 + k]).astype(BF)
        return 0

    copies = []
    for n in range(4):
        lax.fori_loop(4 * n, 4 * n + 4, out_step, 0)
        at = slice(64 * n, 64 * n + 64)
        copies.append(pltpu.make_async_copy(result.at[at], out.at[at], sems.at[n]))
        copies[-1].start()
    for copy in copies:
        copy.wait()


def block(arrays, vectors):
    S = pl.BlockSpec(memory_space=pltpu.SMEM)
    V = pl.BlockSpec(memory_space=pltpu.VMEM)
    return pl.pallas_call(
        block_kernel, name="block", out_shape=jax.ShapeDtypeStruct((256, 24, 128), BF),
        in_specs=[S] * len(vectors) + [V] * len(arrays), out_specs=pl.BlockSpec(memory_space=pl.ANY),
        scratch_shapes=[
            pltpu.VMEM((256, ROWS, 128), BF), pltpu.VMEM((256, 256), F), pltpu.VMEM((256, 256), F),
            pltpu.VMEM((CB * 32, 256), BF), pltpu.VMEM((CB // 2, 224, 256), BF),
            pltpu.VMEM((256, 24, 128), F), pltpu.VMEM((24, 256, 128), BF), pltpu.VMEM((24, 256, 128), F),
            pltpu.VMEM((256, 24, 128), BF), pltpu.SemaphoreType.DMA((4,)),
        ],
        compiler_params=pltpu.CompilerParams(vmem_limit_bytes=30 * MIB),
    )(*vectors, *arrays)


def exchange(to_lower, to_upper, axis, wrap):
    size = lax.axis_size(axis)
    up = [(i, (i + 1) % size) for i in range(size if wrap else size - 1)]
    down = [(j, i) for i, j in up]
    return lax.ppermute(to_upper, axis, up), lax.ppermute(to_lower, axis, down)


def local(state, obs_values, obs_offsets, obs_cell, obs_count, w_in, dw_weight, dw_bias, norm_gain, norm_bias,
          w_up, up_bias, w_down, down_bias, layer_scale):
    row_base = (lax.axis_index("lat") * state.shape[1]).astype(jnp.int32).reshape(1)
    sums, up, down = observation_sums(obs_values, obs_offsets, obs_cell, obs_count, row_base, state)
    above, below = exchange(up, down, "lat", False)
    rows, rims = state_rows(state, sums)
    dw_later, w_up_later, w_down_later, _ = lax.optimization_barrier((dw_weight, w_up, w_down, rows))
    weights = prepare(dw_later, w_in, w_up_later, w_down_later, up_bias)
    rims, (toe, wi, w1, w2, b1, smat) = lax.optimization_barrier((rims, weights))
    edge, left, right = edge_sums(sums, rims, above, below)
    from_left, from_right = exchange(left, right, "lon", True)
    partial = encode(sums, edge, above, below, rows, wi)
    return block(
        (partial, left, right, from_left, from_right, toe, wi, w1, b1, w2, smat),
        (dw_bias, norm_gain, norm_bias, down_bias, layer_scale),
    )


def solution(mesh):
    return jax.shard_map(
        local,
        mesh=mesh,
        in_specs=(
            P(None, "lat", "lon"),
            P(None, ("lat", "lon")),
            P(None, ("lat", "lon")),
            P(("lat", "lon")),
            P(("lat", "lon")),
            P(),
            P(),
            P(),
            P(),
            P(),
            P(),
            P(),
            P(),
            P(),
            P(),
        ),
        out_specs=P(None, "lat", "lon"),
        check_vma=False,
    )
```

profile of v0, /device:TPU:16, one launch (start us, length us, event | category | flops | bytes accessed | tf_op | source)
XLA Modules:
  0.0 54.2 jit_solution(13662557293187535587)
XLA Ops:
  0.0 0.0 copy-start.2
  0.8 0.0 copy-start.5
  0.8 0.0 copy-start.6
  0.8 6.4 %observation_sums.1 = (bf16[32,80,256]{2,1,0:T(8,128)(2,1)}, bf16[1488,128]{1,0:T(8,128)(2,1)}, bf16[1488,128]{1,0:T(8,128)(2,1)}) custom-call(s32[1]{0:T(128)S(6)} %copy.16.count, s32[1]{0:T(128)} %bitcast.row_base, bf16[64,2048]{1,0:T(8,128)(2,1)} %vals_in.1, f32[2,2048]{1,0:T(2,128)} %offs_in.1, s32[1,2048]{1,0:T(1,128)} %bitcast.6, ...), custom_call_target="tpu_custom_call" | custom-call | tf_op jit(solution)/shard_map/observation_sums/pallas_call | solution.py:101
  7.2 0.0 copy-start.7
  7.3 1.9 %collective-permute-start = (bf16[1488,128]{1,0:T(8,128)(2,1)}, bf16[1488,128]{1,0:T(8,128)(2,1)S(1)}, u32[]{:S(2)}, u32[]{:S(2)}) collective-permute-start(bf16[1488,128]{1,0:T(8,128)(2,1)} %get-tuple-element.42), channel_id=1, source_target_pairs={{0,16},{16,32},{32,48},{48,64},{64,80},{80,96},{96,112},{112,128},... | collective-permute-start | bytes 1142792 | tf_op jit(solution)/shard_map/ppermute | solution.py:405
  9.2 4.5 %collective-permute-start.1 = (bf16[1488,128]{1,0:T(8,128)(2,1)}, bf16[1488,128]{1,0:T(8,128)(2,1)S(1)}, u32[]{:S(2)}, u32[]{:S(2)}) collective-permute-start(bf16[1488,128]{1,0:T(8,128)(2,1)} %get-tuple-element.43), channel_id=1, source_target_pairs={{16,0},{32,16},{48,32},{64,48},{80,64},{96,80},{112,96},{128,112},... | collective-permute-start | bytes 1142792 | tf_op jit(solution)/shard_map/ppermute | solution.py:405
  13.7 0.0 copy-done.2
  13.7 0.0 copy-start
  13.8 1.3 %copy-done = bf16[32,80,256]{2,1,0:T(8,128)(2,1)S(1)} copy-done((bf16[32,80,256]{2,1,0:T(8,128)(2,1)S(1)}, bf16[32,80,256]{2,1,0:T(8,128)(2,1)}, u32[]{:S(2)}) %copy-start) | copy-done | bytes 1310744
  15.1 0.0 copy-start.3
  15.1 0.0 copy-start.4
  15.1 0.0 copy-start.1
  15.1 1.4 %state_rows.1 = (bf16[24,256,128]{2,1,0:T(8,128)(2,1)S(1)}, bf16[832,128]{1,0:T(8,128)(2,1)S(1)}) custom-call(bf16[256,24,128]{2,1,0:T(8,128)(2,1)S(1)} %copy-done.2, bf16[32,80,256]{2,1,0:T(8,128)(2,1)S(1)} %copy-done), custom_call_target="tpu_custom_call" | custom-call | flops 10000000 | bytes 8000000 | tf_op jit(solution)/shard_map/state_rows/pallas_call | solution.py:150
  16.5 0.0 copy-done.5
  16.5 0.0 copy-done.6
  16.5 0.0 copy-done.7
  16.5 0.0 copy-done.3
  16.5 0.0 copy-done.4
  16.6 3.6 %prepare.1 = (bf16[128,48,224]{2,1,0:T(8,128)(2,1)S(1)}, bf16[256,80]{1,0:T(8,128)(2,1)S(1)}, bf16[1024,256]{1,0:T(8,128)(2,1)S(1)}, bf16[256,1024]{1,0:T(8,128)...) custom-call(f32[7,7,256]{2,1,0:T(8,128)S(1)} %bitcast.4, bf16[65,256]{1,0:T(8,128)(2,1)S(1)} %copy-done.6, ...), custom_call_target="tpu_custom_call" | custom-call | flops 10000000 | bytes 8000000 | tf_op jit(solution)/shard_map/prepare/pallas_call | solution.py:227
  20.2 0.5 collective-permute-done.above
  20.7 0.0 collective-permute-done.1.below
  20.7 0.0 copy-done.1
  20.7 1.5 %edge_sums.1 = (bf16[16,80,128]{2,1,0:T(8,128)(2,1)S(1)}, bf16[416,128]{1,0:T(8,128)(2,1)S(1)}, bf16[416,128]{1,0:T(8,128)(2,1)S(1)}) custom-call(bf16[32,80,256]{2,1,0:T(8,128)(2,1)S(1)} %copy-done.1, bf16[832,128]{1,0:T(8,128)(2,1)S(1)} %get-tuple-element.41.rims, bf16[1488,128]{1,0:T(8,128)(2,1)S(1)} %collective-permute-done.above, ...), custom_call_target="tpu_custom_call" | custom-call | tf_op jit(solution)/shard_map/edge_sums/pallas_call | solution.py:190
  22.2 7.0 %collective-permute-start.3 = (bf16[416,128]{1,0:T(8,128)(2,1)S(1)}, bf16[416,128]{1,0:T(8,128)(2,1)S(1)}, u32[]{:S(2)}, u32[]{:S(2)}) collective-permute-start(bf16[416,128]{1,0:T(8,128)(2,1)S(1)} %get-tuple-element.46.left), channel_id=1, source_target_pairs={{1,0},{2,1},{3,2},{4,3},{5,4},{6,5},{7,6},{8,7},{9,8},{10,9},{11,1... | collective-permute-start | bytes 319496 | tf_op jit(solution)/shard_map/ppermute | solution.py:405
  29.1 0.0 collective-permute-start.2
  29.1 0.0 copy-start.8
  29.2 0.0 copy-start.9
  29.2 0.0 copy-start.10
  29.2 0.0 copy-start.11
  29.2 0.0 copy-start.12
  29.2 3.3 %encode.1.partial = bf16[256,32,128]{2,1,0:T(8,128)(2,1)S(1)} custom-call(bf16[32,80,256]{2,1,0:T(8,128)(2,1)S(1)} %copy-done.1, bf16[16,80,128]{2,1,0:T(8,128)(2,1)S(1)} %get-tuple-element.44.edge, bf16[1488,128]{1,0:T(8,128)(2,1)S(1)} %collective-permute-done.above, bf16[1488,128]{1,0:T(8,128)(2,1)S(1)} %collective-permute-done.1.below, ...), custom_call_target="tpu_custom_call" | custom-call | flops 100000000 | bytes 8000000 | tf_op jit(solution)/shard_map/encode/pallas_call | solution.py:278
  32.5 0.0 collective-permute-done.3.from_right
  32.5 4.9 %collective-permute-done.2.from_left = bf16[416,128]{1,0:T(8,128)(2,1)S(1)} collective-permute-done((bf16[416,128]{1,0:T(8,128)(2,1)S(1)}, bf16[416,128]{1,0:T(8,128)(2,1)S(1)}, u32[]{:S(2)}, u32[]{:S(2)}) %collective-permute-start.2) | collective-permute-done | bytes 106528 | tf_op jit(solution)/shard_map/ppermute | solution.py:405
  37.5 0.0 copy-done.8
  37.5 0.0 copy-done.9
  37.5 0.0 copy-done.10
  37.5 0.0 copy-done.11
  37.5 0.0 copy-done.12
  37.5 16.7 %block.1 = bf16[256,24,128]{2,1,0:T(8,128)(2,1)} custom-call(f32[256]{0:T(256)S(1)} %copy-done.8, f32[256]{0:T(256)S(1)} %copy-done.9, f32[256]{0:T(256)S(1)} %copy-done.10, f32[256]{0:T(256)S(1)} %copy-done.11, f32[256]{0:T(256)S(1)} %copy-done.12, bf16[256,32,128]{2,1,0:T(8,128)(2,1)S(1)} %encode.1.partial, bf16[416,128]{1,0:T(8,128)(2,1)S(1)} %get-tuple-element.46.left, ...), custom_call_target="tpu_custom_call" | custom-call | tf_op jit(solution)/shard_map/block/pallas_call | solution.py:388
Async XLA Ops:
  0.0 13.7 %copy-start.2 = (bf16[256,24,128]{2,1,0:T(8,128)(2,1)S(1)}, bf16[256,24,128]{2,1,0:T(8,128)(2,1)}, u32[]{:S(2)}) copy-start(bf16[256,24,128]{2,1,0:T(8,128)(2,1)} %state.1) | copy-start | bytes 4718596
  0.8 15.7 %copy-start.5 = (f32[256,7,7]{0,2,1:T(8,128)S(1)}, f32[256,7,7]{0,2,1:T(8,128)}, u32[]{:S(2)}) copy-start(f32[256,7,7]{0,2,1:T(8,128)} %param.21) | copy-start | bytes 150532
  0.8 15.7 %copy-start.6 = (bf16[65,256]{1,0:T(8,128)(2,1)S(1)}, bf16[65,256]{1,0:T(8,128)(2,1)}, u32[]{:S(2)}) copy-start(bf16[65,256]{1,0:T(8,128)(2,1)} %w_in.1) | copy-start | bytes 99844
  7.2 9.3 %copy-start.7 = (f32[1024]{0:T(1024)S(1)}, f32[1024]{0:T(1024)}, u32[]{:S(2)}) copy-start(f32[1024]{0:T(1024)} %param.26) | copy-start | bytes 12292
  7.3 13.4 %collective-permute-start = (bf16[1488,128]{1,0:T(8,128)(2,1)}, bf16[1488,128]{1,0:T(8,128)(2,1)S(1)}, u32[]{:S(2)}, u32[]{:S(2)}) collective-permute-start(bf16[1488,128]{1,0:T(8,128)(2,1)} %get-tuple-element.42), channel_id=1, source_target_pairs={{0,16},{16,32},{32,48},{48,64},{64,80},{80,96},{96,112},{112,128},... | collective-permute-start | bytes 1142792 | tf_op jit(solution)/shard_map/ppermute | solution.py:405
  9.2 11.5 %collective-permute-start.1 = (bf16[1488,128]{1,0:T(8,128)(2,1)}, bf16[1488,128]{1,0:T(8,128)(2,1)S(1)}, u32[]{:S(2)}, u32[]{:S(2)}) collective-permute-start(bf16[1488,128]{1,0:T(8,128)(2,1)} %get-tuple-element.43), channel_id=1, source_target_pairs={{16,0},{32,16},{48,32},{64,48},{80,64},{96,80},{112,96},{128,112},... | collective-permute-start | bytes 1142792 | tf_op jit(solution)/shard_map/ppermute | solution.py:405
  13.7 1.3 %copy-start = (bf16[32,80,256]{2,1,0:T(8,128)(2,1)S(1)}, bf16[32,80,256]{2,1,0:T(8,128)(2,1)}, u32[]{:S(2)}) copy-start(bf16[32,80,256]{2,1,0:T(8,128)(2,1)} %get-tuple-element.29.sums) | copy-start | bytes 3932164
  15.1 1.5 %copy-start.3 = (bf16[256,1024]{1,0:T(8,128)(2,1)S(1)}, bf16[256,1024]{1,0:T(8,128)(2,1)}, u32[]{:S(2)}) copy-start(bf16[256,1024]{1,0:T(8,128)(2,1)} %w_up) | copy-start | bytes 1572868
  15.1 1.5 %copy-start.4 = (bf16[1024,256]{1,0:T(8,128)(2,1)S(1)}, bf16[1024,256]{1,0:T(8,128)(2,1)}, u32[]{:S(2)}) copy-start(bf16[1024,256]{1,0:T(8,128)(2,1)} %w_down) | copy-start | bytes 1572868
  15.1 5.6 %copy-start.1 = (bf16[32,80,256]{2,1,0:T(8,128)(2,1)S(1)}, bf16[32,80,256]{2,1,0:T(8,128)(2,1)}, u32[]{:S(2)}) copy-start(bf16[32,80,256]{2,1,0:T(8,128)(2,1)} %get-tuple-element.29.sums) | copy-start | bytes 3932164
  22.2 10.3 %collective-permute-start.3 = (bf16[416,128]{1,0:T(8,128)(2,1)S(1)}, bf16[416,128]{1,0:T(8,128)(2,1)S(1)}, u32[]{:S(2)}, u32[]{:S(2)}) collective-permute-start(bf16[416,128]{1,0:T(8,128)(2,1)S(1)} %get-tuple-element.46.left), channel_id=1, source_target_pairs={{1,0},{2,1},{3,2},{4,3},{5,4},{6,5},{7,6},{8,7},{9,8},{10,9},{11,1... | collective-permute-start | bytes 319496 | tf_op jit(solution)/shard_map/ppermute | solution.py:405
  29.1 8.3 %collective-permute-start.2 = (bf16[416,128]{1,0:T(8,128)(2,1)S(1)}, bf16[416,128]{1,0:T(8,128)(2,1)S(1)}, u32[]{:S(2)}, u32[]{:S(2)}) collective-permute-start(bf16[416,128]{1,0:T(8,128)(2,1)S(1)} %get-tuple-element.47.right), channel_id=1, source_target_pairs={{0,1},{1,2},{2,3},{3,4},{4,5},{5,6},{6,7},{7,8},{8,9},{9,10},{10,1... | collective-permute-start | bytes 319496 | tf_op jit(solution)/shard_map/ppermute | solution.py:405
  29.1 8.3 %copy-start.8 = (f32[256]{0:T(256)S(1)}, f32[256]{0:T(256)}, u32[]{:S(2)}) copy-start(f32[256]{0:T(256)} %dwb.1) | copy-start | bytes 3076
  29.2 8.3 %copy-start.9 = (f32[256]{0:T(256)S(1)}, f32[256]{0:T(256)}, u32[]{:S(2)}) copy-start(f32[256]{0:T(256)} %gain.1) | copy-start | bytes 3076
  29.2 8.3 %copy-start.10 = (f32[256]{0:T(256)S(1)}, f32[256]{0:T(256)}, u32[]{:S(2)}) copy-start(f32[256]{0:T(256)} %nbias.1) | copy-start | bytes 3076
  29.2 8.3 %copy-start.11 = (f32[256]{0:T(256)S(1)}, f32[256]{0:T(256)}, u32[]{:S(2)}) copy-start(f32[256]{0:T(256)} %db.1) | copy-start | bytes 3076
  29.2 8.3 %copy-start.12 = (f32[256]{0:T(256)S(1)}, f32[256]{0:T(256)}, u32[]{:S(2)}) copy-start(f32[256]{0:T(256)} %ls.1) | copy-start | bytes 3076
where the time goes:
time: 55.1 us; the launch traced here: 54.2 us
  Pallas kernels  33 us (60%)
  starting transfers between devices  13.4 us (24%)
  waiting for transfers between devices  5.43 us (10%)
  local copies, waits for them, and re-layouts  1.36 us (2%)
  between operations  0.96 us (2%)
    pallas_call x1, Pallas kernels, block(): pl.pallas_call(block_kernel, name='block', out_shape=jax.ShapeDtypeStruct...  16.7 us
    ppermute x2, starting transfers between devices, exchange(): lax.ppermute(to_lower, axis, down)  11.5 us
    pallas_call x1, Pallas kernels, observation_sums(): pl.pallas_call(sums_kernel, name='observation_sums', out_shape=(shape((RO...  6.44 us
    ppermute x2, waiting for transfers between devices, exchange(): lax.ppermute(to_upper, axis, up)  5.42 us
    pallas_call x1, Pallas kernels, prepare(): pl.pallas_call(prepare_kernel, name='prepare', out_shape=(shape((128, 48,...  3.61 us
    pallas_call x1, Pallas kernels, encode(): pl.pallas_call(encode_kernel, name='encode', out_shape=jax.ShapeDtypeStru...  3.32 us
    ppermute x2, starting transfers between devices, exchange(): lax.ppermute(to_upper, axis, up)  1.92 us
    pallas_call x1, Pallas kernels, edge_sums(): pl.pallas_call(edge_kernel, name='edge_sums', out_shape=(shape((16, SRC,...  1.51 us
  transfers between devices with their start and end apart: 4, of which 2 were waited for; matrix products, arithmetic and copies ran while one was open for 0% of the time, Pallas kernels for 15%

commit v1 on v0

--- a/solution.py
+++ b/solution.py
@@ -28,8 +28,17 @@
     return lax.broadcasted_iota(jnp.int32, (rows, 128), 1)
 
 
-def sums_kernel(count, row_base, vals_in, offs_in, cell_in, state_in, sums, up, down, vals, offs, cell, state, scaled, acc, sems):
+def even(index):
+    return (index[0] & 1) == 0
+
+
+def pick(condition, a, b, at):
+    return jnp.where(condition, a[at].astype(F), b[at].astype(F))
+
+
+def sums_kernel(count, lat, vals_in, offs_in, cell_in, state_in, sums, out_a, out_b, vals, offs, cell, state, scaled, acc, sems):
     live_count = count[0]
+    row_base = lat[0] * 24
     copies = [
         pltpu.make_async_copy(vals_in, vals, sems.at[0]),
         pltpu.make_async_copy(offs_in, offs, sems.at[1]),
@@ -59,7 +68,7 @@
             return jnp.where(inside, jnp.exp(-spread * spread * inverse_width), 0.0)
 
         place = lax.broadcasted_iota(jnp.int32, (ROWS, OBS_BLOCK), 0) - W
-        on_grid = (place + row_base[0] >= 0) & (place + row_base[0] < GRID_ROWS)
+        on_grid = (place + row_base >= 0) & (place + row_base < GRID_ROWS)
         lat_weight = weight(offs[0:1, ks], place, row, on_grid)
         place = lax.broadcasted_iota(jnp.int32, (136, OBS_BLOCK), 0)
         first = weight(offs[1:2, ks], place, col, place < 128 + W)
@@ -80,21 +89,30 @@
         copy.wait()
     for p in range(ROWS):
         sums[p] = acc[p * SRC:(p + 1) * SRC].astype(BF)
-    for msg, first, state_tile, state_row in ((up, 0, 0, 0), (down, 24, 8, 5)):
-        side = jnp.zeros((SRC, 128), F)
-        for i in range(8):
-            part = acc[(first + i) * SRC:(first + i + 1) * SRC]
-            msg[i * SRC:(i + 1) * SRC] = part[:, :128].astype(BF)
-            moved = pltpu.roll(part[:, 128:], i * 8 + 4, 1)
-            side = jnp.where((lanes(SRC) >> 3) == i, moved, side)
-        msg[8 * SRC:9 * SRC] = side.astype(BF)
-        for c in range(0, 256, 16):
-            x = jnp.swapaxes(state[c:c + 16, state_tile:state_tile + 8, :].astype(F), 0, 1).astype(BF)
-            for j in range(3):
-                msg[LAT_STATE + j * 256 + c:LAT_STATE + j * 256 + c + 16] = x[state_row + j]
-
-
-def observation_sums(obs_values, obs_offsets, obs_cell, obs_count, row_base, state):
+    def fill(up, down):
+        for msg, first, state_tile, state_row in ((up, 0, 0, 0), (down, 24, 8, 5)):
+            side = jnp.zeros((SRC, 128), F)
+            for i in range(8):
+                part = acc[(first + i) * SRC:(first + i + 1) * SRC]
+                msg[i * SRC:(i + 1) * SRC] = part[:, :128].astype(BF)
+                moved = pltpu.roll(part[:, 128:], i * 8 + 4, 1)
+                side = jnp.where((lanes(SRC) >> 3) == i, moved, side)
+            msg[8 * SRC:9 * SRC] = side.astype(BF)
+            for c in range(0, 256, 16):
+                x = jnp.swapaxes(state[c:c + 16, state_tile:state_tile + 8, :].astype(F), 0, 1).astype(BF)
+                for j in range(3):
+                    msg[LAT_STATE + j * 256 + c:LAT_STATE + j * 256 + c + 16] = x[state_row + j]
+
+    @pl.when(even(lat))
+    def _():
+        fill(out_b, out_a)
+
+    @pl.when(jnp.logical_not(even(lat)))
+    def _():
+        fill(out_a, out_b)
+
+
+def observation_sums(obs_values, obs_offsets, obs_cell, obs_count, lat, state):
     S = pl.BlockSpec(memory_space=pltpu.SMEM)
     V = pl.BlockSpec(memory_space=pltpu.VMEM)
     shape = jax.ShapeDtypeStruct
@@ -107,7 +125,7 @@
             pltpu.VMEM((ROWS * SRC, OBS_BLOCK), BF), pltpu.VMEM((ROWS * SRC, 256), F), pltpu.SemaphoreType.DMA((5,)),
         ],
         compiler_params=pltpu.CompilerParams(vmem_limit_bytes=56 * MIB),
-    )(obs_count, row_base, obs_values, obs_offsets, obs_cell.reshape(1, -1), state)
+    )(obs_count, lat, obs_values, obs_offsets, obs_cell.reshape(1, -1), state)
 
 
 def place(p):
@@ -154,21 +172,28 @@
     )(state, sums)
 
 
-def edge_kernel(sums, rims, above, below, edge, left, right):
+def edge_kernel(lat, lon, sums, rims, in_a, in_b, edge, out_a, out_b):
+    lat_even, lon_even = even(lat), even(lon)
+    above = lambda at: pick(lat_even, in_b, in_a, at)
+    below = lambda at: pick(lat_even, in_a, in_b, at)
+
+    def store(at, left, right):
+        out_a[at] = jnp.where(lon_even, right, left).astype(BF)
+        out_b[at] = jnp.where(lon_even, left, right).astype(BF)
+
     lane = lanes(SRC)
     outer = (lane < 4) | (lane >= 124)
     packed = [[rims[first + k * SRC:first + (k + 1) * SRC].astype(F) for k in range(2)] for first in (0, RIMS)]
     for e in range(16):
         p = e if e < 8 else e + 16
         msg, i = (above, p) if p < 8 else (below, p - 24)
-        moved = pltpu.roll(msg[8 * SRC:9 * SRC].astype(F), 124 - i * 8, 1)
-        main = sums[p, :, :128].astype(F) + msg[i * SRC:(i + 1) * SRC].astype(F)
+        moved = pltpu.roll(msg(slice(8 * SRC, 9 * SRC)), 124 - i * 8, 1)
+        main = sums[p, :, :128].astype(F) + msg(slice(i * SRC, (i + 1) * SRC))
         side = sums[p, :, 128:].astype(F) + jnp.where(outer, moved, 0.0)
         edge[e] = main.astype(BF)
         pack(packed, p, main, side)
     for k in range(2):
-        left[k * SRC:(k + 1) * SRC] = packed[0][k].astype(BF)
-        right[k * SRC:(k + 1) * SRC] = packed[1][k].astype(BF)
+        store(slice(k * SRC, (k + 1) * SRC), packed[0][k], packed[1][k])
     early = (lanes(64) & 7) < 4
     for c in range(0, 256, 64):
         halves = []
@@ -177,21 +202,24 @@
             out = rims[at:at + 64].astype(F)
             for j in range(3):
                 p = first + j
-                x = msg[LAT_STATE + j * 256 + c:LAT_STATE + j * 256 + c + 64].astype(F)
+                x = msg(slice(LAT_STATE + j * 256 + c, LAT_STATE + j * 256 + c + 64))
                 out = jnp.where((lanes(64) >> 3) == place(p), pltpu.roll(x, place(p) * 8 + 4, 1), out)
             halves.append(out)
         at = slice(LON_STATE + c, LON_STATE + c + 64)
-        left[at] = jnp.where(early, pltpu.roll(halves[1], 124, 1), halves[0]).astype(BF)
-        right[at] = jnp.where(early, halves[0], pltpu.roll(halves[1], 4, 1)).astype(BF)
-
-
-def edge_sums(sums, rims, above, below):
+        store(
+            at,
+            jnp.where(early, pltpu.roll(halves[1], 124, 1), halves[0]),
+            jnp.where(early, halves[0], pltpu.roll(halves[1], 4, 1)),
+        )
+
+
+def edge_sums(*arrays):
     shape = jax.ShapeDtypeStruct
     return pl.pallas_call(
-        edge_kernel, name="edge_sums",
+        edge_kernel, name="edge_sums", in_specs=[pl.BlockSpec(memory_space=pltpu.SMEM)] * 2 + [pl.BlockSpec(memory_space=pltpu.VMEM)] * 4,
         out_shape=(shape((16, SRC, 128), BF), shape((LON_MSG, 128), BF), shape((LON_MSG, 128), BF)),
         compiler_params=pltpu.CompilerParams(vmem_limit_bytes=16 * MIB),
-    )(sums, rims, above, below)
+    )(*arrays)
 
 
 def prepare_kernel(taps, w_in, w_up, w_down, b1, toe, wi, w1, w2, b1c, smat, padded, base):
@@ -243,7 +271,9 @@
     return jnp.where(col == out % 128 + d, 1.0, 0.0).astype(BF)
 
 
-def encode_kernel(sums, edge, above, below, rows, wi, native, mixed):
+def encode_kernel(lat, sums, edge, in_a, in_b, rows, wi, native, mixed):
+    lat_even = even(lat)
+
     def encode(*cases):
         both = jnp.dot(wi[...], jnp.concatenate([main for _, main, _ in cases], 1), preferred_element_type=F)
         for n, (p, _, state) in enumerate(cases):
@@ -253,7 +283,7 @@
     mixed[31] = jnp.zeros((256, 128), BF)
     for j in range(3):
         at = slice(LAT_STATE + j * 256, LAT_STATE + j * 256 + 256)
-        encode((1 + j, edge[1 + j], above[at]), (28 + j, edge[12 + j], below[at]))
+        encode((1 + j, edge[1 + j], pick(lat_even, in_b, in_a, at)), (28 + j, edge[12 + j], pick(lat_even, in_a, in_b, at)))
 
     def edge_row(j, _):
         encode((4 + j, edge[4 + j], rows[j]), (24 + j, edge[8 + j], rows[20 + j]))
@@ -276,25 +306,28 @@
 
 def encode(*arrays):
     return pl.pallas_call(
-        encode_kernel, name="encode", out_shape=jax.ShapeDtypeStruct((256, ROWS, 128), BF),
+        encode_kernel, name="encode", in_specs=[pl.BlockSpec(memory_space=pltpu.SMEM)] + [pl.BlockSpec(memory_space=pltpu.VMEM)] * 6,
+        out_shape=jax.ShapeDtypeStruct((256, ROWS, 128), BF),
         scratch_shapes=[pltpu.VMEM((ROWS, 256, 128), BF)],
         cost_estimate=pl.CostEstimate(flops=10**8, bytes_accessed=8 * 10**6, transcendentals=0),
         compiler_params=pltpu.CompilerParams(vmem_limit_bytes=20 * MIB),
     )(*arrays)
 
 
-def block_kernel(dwb, gain, nbias, db, ls, partial, left, right, from_left, from_right,
+def block_kernel(lon, dwb, gain, nbias, db, ls, partial, out_a, out_b, in_a, in_b,
                  toe, wi, w1, b1, w2, smat, out, native, sides, inward, mext, xs, filt, xbuf, obuf, result, sems):
+    lon_even = even(lon)
     first = (lanes(SRC) & 7) < 4
     parts = []
     for k in range(2):
         at = slice(k * SRC, (k + 1) * SRC)
-        a, b = from_left[at].astype(F), from_right[at].astype(F)
-        parts.append(jnp.where(first, left[at].astype(F) + a, right[at].astype(F) + b))
+        a, b = pick(lon_even, in_b, in_a, at), pick(lon_even, in_a, in_b, at)
+        parts.append(jnp.where(first, pick(lon_even, out_b, out_a, at) + a, pick(lon_even, out_a, out_b, at) + b))
         parts.append(jnp.where(first, b, a))
     both = jnp.dot(wi[...], jnp.concatenate(parts, 1).astype(BF), preferred_element_type=F)
     first = (lanes(256) & 7) < 4
-    a, b = from_left[LON_STATE:LON_STATE + 256].astype(F), from_right[LON_STATE:LON_STATE + 256].astype(F)
+    at = slice(LON_STATE, LON_STATE + 256)
+    a, b = pick(lon_even, in_b, in_a, at), pick(lon_even, in_a, in_b, at)
     rims = (jnp.where(first, a, b), jnp.where(first, pltpu.roll(a, 124, 1), pltpu.roll(b, 4, 1)))
     for k in range(2):
         sides[:, k * 128:(k + 1) * 128] = (both[:, 2 * k * 128:(2 * k + 1) * 128] + rims[k]).astype(BF).astype(F)
@@ -398,28 +431,30 @@
     )(*vectors, *arrays)
 
 
-def exchange(to_lower, to_upper, axis, wrap):
+def exchange(a, b, axis, wrap):
     size = lax.axis_size(axis)
-    up = [(i, (i + 1) % size) for i in range(size if wrap else size - 1)]
-    down = [(j, i) for i, j in up]
-    return lax.ppermute(to_upper, axis, up), lax.ppermute(to_lower, axis, down)
+    first = [(i, i + 1) for i in range(0, size, 2)]
+    second = [(i, (i + 1) % size) for i in range(1, size if wrap else size - 1, 2)]
+    swap = lambda x, pairs: lax.ppermute(x, axis, pairs + [(j, i) for i, j in pairs])
+    return swap(a, first), swap(b, second)
 
 
 def local(state, obs_values, obs_offsets, obs_cell, obs_count, w_in, dw_weight, dw_bias, norm_gain, norm_bias,
           w_up, up_bias, w_down, down_bias, layer_scale):
-    row_base = (lax.axis_index("lat") * state.shape[1]).astype(jnp.int32).reshape(1)
-    sums, up, down = observation_sums(obs_values, obs_offsets, obs_cell, obs_count, row_base, state)
-    above, below = exchange(up, down, "lat", False)
+    lat = lax.axis_index("lat").astype(jnp.int32).reshape(1)
+    lon = lax.axis_index("lon").astype(jnp.int32).reshape(1)
+    sums, lat_a, lat_b = observation_sums(obs_values, obs_offsets, obs_cell, obs_count, lat, state)
+    lat_a, lat_b = exchange(lat_a, lat_b, "lat", False)
     rows, rims = state_rows(state, sums)
     dw_later, w_up_later, w_down_later, _ = lax.optimization_barrier((dw_weight, w_up, w_down, rows))
     weights = prepare(dw_later, w_in, w_up_later, w_down_later, up_bias)
     rims, (toe, wi, w1, w2, b1, smat) = lax.optimization_barrier((rims, weights))
-    edge, left, right = edge_sums(sums, rims, above, below)
-    from_left, from_right = exchange(left, right, "lon", True)
-    partial = encode(sums, edge, above, below, rows, wi)
+    edge, lon_a, lon_b = edge_sums(lat, lon, sums, rims, lat_a, lat_b)
+    from_a, from_b = exchange(lon_a, lon_b, "lon", True)
+    partial = encode(lat, sums, edge, lat_a, lat_b, rows, wi)
     return block(
-        (partial, left, right, from_left, from_right, toe, wi, w1, b1, w2, smat),
-        (dw_bias, norm_gain, norm_bias, down_bias, layer_scale),
+        (partial, lon_a, lon_b, from_a, from_b, toe, wi, w1, b1, w2, smat),
+        (lon, dw_bias, norm_gain, norm_bias, down_bias, layer_scale),
     )
 
 

time: 55.1 us -> 51.8 us (0.940)
  the two profiles are of different devices: /device:TPU:16 before, /device:TPU:1 now
where the time goes in v1:
time: 51.8 us; the launch traced here: 52 us
  Pallas kernels  30.5 us (59%)
  starting transfers between devices  16.8 us (32%)
  waiting for transfers between devices  2.28 us (4%)
  local copies, waits for them, and re-layouts  1.36 us (3%)
  between operations  0.98 us (2%)
    pallas_call x1, Pallas kernels, block(): pl.pallas_call(block_kernel, name='block', out_shape=jax.ShapeDtypeStruct...  16.9 us
    ppermute x4, starting transfers between devices, exchange(): lax.ppermute(x, axis, pairs + [(j, i) for i, j in pairs])  16.8 us
    pallas_call x1, Pallas kernels, observation_sums(): pl.pallas_call(sums_kernel, name='observation_sums', out_shape=(shape((RO...  3.77 us
    pallas_call x1, Pallas kernels, prepare(): pl.pallas_call(prepare_kernel, name='prepare', out_shape=(shape((128, 48,...  3.61 us
    pallas_call x1, Pallas kernels, encode(): pl.pallas_call(encode_kernel, name='encode', in_specs=[pl.BlockSpec(memor...  3.34 us
    ppermute x4, waiting for transfers between devices, exchange(): lax.ppermute(x, axis, pairs + [(j, i) for i, j in pairs])  2.28 us
    pallas_call x1, Pallas kernels, edge_sums(): pl.pallas_call(edge_kernel, name='edge_sums', in_specs=[pl.BlockSpec(memo...  1.52 us
    pallas_call x1, Pallas kernels, state_rows(): pl.pallas_call(rows_kernel, name='state_rows', out_shape=(shape((24, 256,...  1.43 us
  transfers between devices with their start and end apart: 4, of which 1 were waited for; matrix products, arithmetic and copies ran while one was open for 0% of the time, Pallas kernels for 16%

profile of v1, /device:TPU:1, one launch (start us, length us, event | category | flops | bytes accessed | tf_op | source)
XLA Modules:
  0.0 52.0 jit_solution(5487564737565675353)
XLA Ops:
  0.0 0.0 copy-start.2
  0.8 0.0 copy-start.5
  0.8 0.0 copy-start.6
  0.8 3.8 %observation_sums.1 = (bf16[32,80,256]{2,1,0:T(8,128)(2,1)}, bf16[1488,128]{1,0:T(8,128)(2,1)}, bf16[1488,128]{1,0:T(8,128)(2,1)}) custom-call(s32[1]{0:T(128)S(6)} %copy.16.count, s32[1]{0:T(128)} %bitcast.1.lat, bf16[64,2048]{1,0:T(8,128)(2,1)} %vals_in.1, f32[2,2048]{1,0:T(2,128)} %offs_in.1, s32[1,2048]{1,0:T(1,128)} %bitcast.7, bf16[256,24,128]{2,1,0:T(8,128)(2,1)} %state.1), custom_call_target="tpu_custom_call" | custom-call | tf_op jit(solution)/shard_map/observation_sums/pallas_call | solution.py:119
  4.6 0.0 copy-start.7
  4.6 3.3 %collective-permute-start = (bf16[1488,128]{1,0:T(8,128)(2,1)}, bf16[1488,128]{1,0:T(8,128)(2,1)S(1)}, u32[]{:S(2)}, u32[]{:S(2)}) collective-permute-start(bf16[1488,128]{1,0:T(8,128)(2,1)} %get-tuple-element.42), channel_id=1, source_target_pairs={{0,16},{32,48},{64,80},{96,112},{128,144},{160,176},{192,208},{224... | collective-permute-start | bytes 1142792 | tf_op jit(solution)/shard_map/ppermute | solution.py:438
  7.9 4.0 %collective-permute-start.1 = (bf16[1488,128]{1,0:T(8,128)(2,1)}, bf16[1488,128]{1,0:T(8,128)(2,1)S(1)}, u32[]{:S(2)}, u32[]{:S(2)}) collective-permute-start(bf16[1488,128]{1,0:T(8,128)(2,1)} %get-tuple-element.43), channel_id=1, source_target_pairs={{16,32},{48,64},{80,96},{112,128},{144,160},{176,192},{208,224},{3... | collective-permute-start | bytes 1142792 | tf_op jit(solution)/shard_map/ppermute | solution.py:438
  11.9 0.0 copy-done.2
  11.9 0.0 copy-start
  11.9 1.3 %copy-done = bf16[32,80,256]{2,1,0:T(8,128)(2,1)S(1)} copy-done((bf16[32,80,256]{2,1,0:T(8,128)(2,1)S(1)}, bf16[32,80,256]{2,1,0:T(8,128)(2,1)}, u32[]{:S(2)}) %copy-start) | copy-done | bytes 1310744
  13.2 0.0 copy-start.3
  13.2 0.0 copy-start.4
  13.2 0.0 copy-start.1
  13.2 1.4 %state_rows.1 = (bf16[24,256,128]{2,1,0:T(8,128)(2,1)S(1)}, bf16[832,128]{1,0:T(8,128)(2,1)S(1)}) custom-call(bf16[256,24,128]{2,1,0:T(8,128)(2,1)S(1)} %copy-done.2, bf16[32,80,256]{2,1,0:T(8,128)(2,1)S(1)} %copy-done), custom_call_target="tpu_custom_call" | custom-call | flops 10000000 | bytes 8000000 | tf_op jit(solution)/shard_map/state_rows/pallas_call | solution.py:168
  14.7 0.0 copy-done.5
  14.7 0.0 copy-done.6
  14.7 0.0 copy-done.7
  14.7 0.0 copy-done.3
  14.7 0.0 copy-done.4
  14.7 3.6 %prepare.1 = (bf16[128,48,224]{2,1,0:T(8,128)(2,1)S(1)}, bf16[256,80]{1,0:T(8,128)(2,1)S(1)}, bf16[1024,256]{1,0:T(8,128)(2,1)S(1)}, bf16[256,1024]{1,0:T(8,128)...) custom-call(f32[7,7,256]{2,1,0:T(8,128)S(1)} %bitcast.5, bf16[65,256]{1,0:T(8,128)(2,1)S(1)} %copy-done.6, ...), custom_call_target="tpu_custom_call" | custom-call | flops 10000000 | bytes 8000000 | tf_op jit(solution)/shard_map/prepare/pallas_call | solution.py:255
  18.3 0.0 collective-permute-done.in_a
  18.3 2.3 %collective-permute-done.1.in_b = bf16[1488,128]{1,0:T(8,128)(2,1)S(1)} collective-permute-done((bf16[1488,128]{1,0:T(8,128)(2,1)}, bf16[1488,128]{1,0:T(8,128)(2,1)S(1)}, u32[]{:S(2)}, u32[]{:S(2)}) %collective-permute-start.1) | collective-permute-done | bytes 380960 | tf_op jit(solution)/shard_map/ppermute | solution.py:438
  20.6 0.0 copy-done.1
  20.6 1.5 %edge_sums.1 = (bf16[16,80,128]{2,1,0:T(8,128)(2,1)S(1)}, bf16[416,128]{1,0:T(8,128)(2,1)S(1)}, bf16[416,128]{1,0:T(8,128)(2,1)S(1)}) custom-call(s32[1]{0:T(128)} %bitcast.1.lat, s32[1]{0:T(128)} %bitcast.lon, bf16[32,80,256]{2,1,0:T(8,128)(2,1)S(1)} %copy-done.1, bf16[832,128]{1,0:T(8,128)(2,1)S(1)} %get-tuple-element.41.rims, ...), custom_call_target="tpu_custom_call" | custom-call | tf_op jit(solution)/shard_map/edge_sums/pallas_call | solution.py:218
  22.1 1.7 %collective-permute-start.2 = (bf16[416,128]{1,0:T(8,128)(2,1)S(1)}, bf16[416,128]{1,0:T(8,128)(2,1)S(1)}, u32[]{:S(2)}, u32[]{:S(2)}) collective-permute-start(bf16[416,128]{1,0:T(8,128)(2,1)S(1)} %get-tuple-element.46.out_a), channel_id=1, source_target_pairs={{0,1},{2,3},{4,5},{6,7},{8,9},{10,11},{12,13},{14,15},{1,0},{3,2},... | collective-permute-start | bytes 319496 | tf_op jit(solution)/shard_map/ppermute | solution.py:438
  23.9 7.8 %collective-permute-start.3 = (bf16[416,128]{1,0:T(8,128)(2,1)S(1)}, bf16[416,128]{1,0:T(8,128)(2,1)S(1)}, u32[]{:S(2)}, u32[]{:S(2)}) collective-permute-start(bf16[416,128]{1,0:T(8,128)(2,1)S(1)} %get-tuple-element.47.out_b), channel_id=1, source_target_pairs={{1,2},{3,4},{5,6},{7,8},{9,10},{11,12},{13,14},{15,0},{2,1},{4,3},... | collective-permute-start | bytes 319496 | tf_op jit(solution)/shard_map/ppermute | solution.py:438
  31.7 0.0 copy-start.8
  31.7 0.0 copy-start.9
  31.7 0.0 copy-start.10
  31.7 0.0 copy-start.11
  31.7 0.0 copy-start.12
  31.7 3.3 %encode.1.partial = bf16[256,32,128]{2,1,0:T(8,128)(2,1)S(1)} custom-call(s32[1]{0:T(128)} %bitcast.1.lat, bf16[32,80,256]{2,1,0:T(8,128)(2,1)S(1)} %copy-done.1, bf16[16,80,128]{2,1,0:T(8,128)(2,1)S(1)} %get-tuple-element.44.edge, bf16[1488,128]{1,0:T(8,128)(2,1)S(1)} %collective-permute-done.in_a, bf16[1488,128]{1,0:T(8,128)(2,1)S(1)} %collective-permute-done.1.in_b, ...), custom_call_target="tpu_custom_call" | custom-call | flops 100000000 | bytes 8000000 | tf_op jit(solution)/shard_map/encode/pallas_call | solution.py:308
  35.0 0.0 collective-permute-done.2.in_a
  35.0 0.0 collective-permute-done.3.in_b
  35.1 0.0 copy-done.8
  35.1 0.0 copy-done.9
  35.1 0.0 copy-done.10
  35.1 0.0 copy-done.11
  35.1 0.0 copy-done.12
  35.1 16.9 %block.1 = bf16[256,24,128]{2,1,0:T(8,128)(2,1)} custom-call(s32[1]{0:T(128)} %bitcast.lon, f32[256]{0:T(256)S(1)} %copy-done.8, f32[256]{0:T(256)S(1)} %copy-done.9, f32[256]{0:T(256)S(1)} %copy-done.10, f32[256]{0:T(256)S(1)} %copy-done.11, f32[256]{0:T(256)S(1)} %copy-done.12, bf16[256,32,128]{2,1,0:T(8,128)(2,1)S(1)} %encode.1.partial, ...), custom_call_target="tpu_custom_call" | custom-call | tf_op jit(solution)/shard_map/block/pallas_call | solution.py:421
Async XLA Ops:
  0.0 11.9 %copy-start.2 = (bf16[256,24,128]{2,1,0:T(8,128)(2,1)S(1)}, bf16[256,24,128]{2,1,0:T(8,128)(2,1)}, u32[]{:S(2)}) copy-start(bf16[256,24,128]{2,1,0:T(8,128)(2,1)} %state.1) | copy-start | bytes 4718596
  0.8 13.9 %copy-start.5 = (f32[256,7,7]{0,2,1:T(8,128)S(1)}, f32[256,7,7]{0,2,1:T(8,128)}, u32[]{:S(2)}) copy-start(f32[256,7,7]{0,2,1:T(8,128)} %param.21) | copy-start | bytes 150532
  0.8 13.9 %copy-start.6 = (bf16[65,256]{1,0:T(8,128)(2,1)S(1)}, bf16[65,256]{1,0:T(8,128)(2,1)}, u32[]{:S(2)}) copy-start(bf16[65,256]{1,0:T(8,128)(2,1)} %w_in.1) | copy-start | bytes 99844
  4.6 10.1 %copy-start.7 = (f32[1024]{0:T(1024)S(1)}, f32[1024]{0:T(1024)}, u32[]{:S(2)}) copy-start(f32[1024]{0:T(1024)} %param.26) | copy-start | bytes 12292
  4.6 13.8 %collective-permute-start = (bf16[1488,128]{1,0:T(8,128)(2,1)}, bf16[1488,128]{1,0:T(8,128)(2,1)S(1)}, u32[]{:S(2)}, u32[]{:S(2)}) collective-permute-start(bf16[1488,128]{1,0:T(8,128)(2,1)} %get-tuple-element.42), channel_id=1, source_target_pairs={{0,16},{32,48},{64,80},{96,112},{128,144},{160,176},{192,208},{224... | collective-permute-start | bytes 1142792 | tf_op jit(solution)/shard_map/ppermute | solution.py:438
  7.9 12.7 %collective-permute-start.1 = (bf16[1488,128]{1,0:T(8,128)(2,1)}, bf16[1488,128]{1,0:T(8,128)(2,1)S(1)}, u32[]{:S(2)}, u32[]{:S(2)}) collective-permute-start(bf16[1488,128]{1,0:T(8,128)(2,1)} %get-tuple-element.43), channel_id=1, source_target_pairs={{16,32},{48,64},{80,96},{112,128},{144,160},{176,192},{208,224},{3... | collective-permute-start | bytes 1142792 | tf_op jit(solution)/shard_map/ppermute | solution.py:438
  11.9 1.3 %copy-start = (bf16[32,80,256]{2,1,0:T(8,128)(2,1)S(1)}, bf16[32,80,256]{2,1,0:T(8,128)(2,1)}, u32[]{:S(2)}) copy-start(bf16[32,80,256]{2,1,0:T(8,128)(2,1)} %get-tuple-element.29.sums) | copy-start | bytes 3932164
  13.2 1.5 %copy-start.3 = (bf16[256,1024]{1,0:T(8,128)(2,1)S(1)}, bf16[256,1024]{1,0:T(8,128)(2,1)}, u32[]{:S(2)}) copy-start(bf16[256,1024]{1,0:T(8,128)(2,1)} %w_up) | copy-start | bytes 1572868
  13.2 1.5 %copy-start.4 = (bf16[1024,256]{1,0:T(8,128)(2,1)S(1)}, bf16[1024,256]{1,0:T(8,128)(2,1)}, u32[]{:S(2)}) copy-start(bf16[1024,256]{1,0:T(8,128)(2,1)} %w_down) | copy-start | bytes 1572868
  13.2 7.4 %copy-start.1 = (bf16[32,80,256]{2,1,0:T(8,128)(2,1)S(1)}, bf16[32,80,256]{2,1,0:T(8,128)(2,1)}, u32[]{:S(2)}) copy-start(bf16[32,80,256]{2,1,0:T(8,128)(2,1)} %get-tuple-element.29.sums) | copy-start | bytes 3932164
  22.1 12.9 %collective-permute-start.2 = (bf16[416,128]{1,0:T(8,128)(2,1)S(1)}, bf16[416,128]{1,0:T(8,128)(2,1)S(1)}, u32[]{:S(2)}, u32[]{:S(2)}) collective-permute-start(bf16[416,128]{1,0:T(8,128)(2,1)S(1)} %get-tuple-element.46.out_a), channel_id=1, source_target_pairs={{0,1},{2,3},{4,5},{6,7},{8,9},{10,11},{12,13},{14,15},{1,0},{3,2},... | collective-permute-start | bytes 319496 | tf_op jit(solution)/shard_map/ppermute | solution.py:438
  23.9 11.2 %collective-permute-start.3 = (bf16[416,128]{1,0:T(8,128)(2,1)S(1)}, bf16[416,128]{1,0:T(8,128)(2,1)S(1)}, u32[]{:S(2)}, u32[]{:S(2)}) collective-permute-start(bf16[416,128]{1,0:T(8,128)(2,1)S(1)} %get-tuple-element.47.out_b), channel_id=1, source_target_pairs={{1,2},{3,4},{5,6},{7,8},{9,10},{11,12},{13,14},{15,0},{2,1},{4,3},... | collective-permute-start | bytes 319496 | tf_op jit(solution)/shard_map/ppermute | solution.py:438
  31.7 3.4 %copy-start.8 = (f32[256]{0:T(256)S(1)}, f32[256]{0:T(256)}, u32[]{:S(2)}) copy-start(f32[256]{0:T(256)} %dwb.1) | copy-start | bytes 3076
  31.7 3.4 %copy-start.9 = (f32[256]{0:T(256)S(1)}, f32[256]{0:T(256)}, u32[]{:S(2)}) copy-start(f32[256]{0:T(256)} %gain.1) | copy-start | bytes 3076
  31.7 3.4 %copy-start.10 = (f32[256]{0:T(256)S(1)}, f32[256]{0:T(256)}, u32[]{:S(2)}) copy-start(f32[256]{0:T(256)} %nbias.1) | copy-start | bytes 3076
  31.7 3.4 %copy-start.11 = (f32[256]{0:T(256)S(1)}, f32[256]{0:T(256)}, u32[]{:S(2)}) copy-start(f32[256]{0:T(256)} %db.1) | copy-start | bytes 3076
  31.7 3.4 %copy-start.12 = (f32[256]{0:T(256)S(1)}, f32[256]{0:T(256)}, u32[]{:S(2)}) copy-start(f32[256]{0:T(256)} %ls.1) | copy-start | bytes 3076

commit v2 on v1

--- a/solution.py
+++ b/solution.py
@@ -10,7 +10,7 @@
 ROWS = 32
 OBS_BLOCK = 512
 GRID_ROWS = 384
-CB = 64
+CB = 128
 RB = 8
 BF = jnp.bfloat16
 F = jnp.float32
@@ -395,7 +395,7 @@
             obuf[i * RB + k] = o[:, k * 128:(k + 1) * 128]
         return 0
 
-    lax.fori_loop(0, 24 // RB, mlp_step, 0)
+    lax.fori_loop(0, 24 // RB, mlp_step, 0, unroll=3)
 
     def out_step(i, _):
         c0 = pl.multiple_of(i * 16, 16)

time: 51.8 us -> 51.6 us (level)
  the two profiles are of different devices: /device:TPU:1 before, /device:TPU:24 now
where the time goes in v2:
time: 51.6 us
  Pallas kernels  32.6 us (63%)
  starting transfers between devices  12.7 us (25%)
  waiting for transfers between devices  3.82 us (7%)
  local copies, waits for them, and re-layouts  1.36 us (3%)
  between operations  1.15 us (2%)
    pallas_call x1, Pallas kernels, block(): pl.pallas_call(block_kernel, name='block', out_shape=jax.ShapeDtypeStruct...  16 us
    ppermute x4, starting transfers between devices, exchange(): lax.ppermute(x, axis, pairs + [(j, i) for i, j in pairs])  12.7 us
    pallas_call x1, Pallas kernels, observation_sums(): pl.pallas_call(sums_kernel, name='observation_sums', out_shape=(shape((RO...  6.64 us
    ppermute x4, waiting for transfers between devices, exchange(): lax.ppermute(x, axis, pairs + [(j, i) for i, j in pairs])  3.82 us
    pallas_call x1, Pallas kernels, prepare(): pl.pallas_call(prepare_kernel, name='prepare', out_shape=(shape((128, 48,...  3.61 us
    pallas_call x1, Pallas kernels, encode(): pl.pallas_call(encode_kernel, name='encode', in_specs=[pl.BlockSpec(memor...  3.32 us
    pallas_call x1, Pallas kernels, edge_sums(): pl.pallas_call(edge_kernel, name='edge_sums', in_specs=[pl.BlockSpec(memo...  1.52 us
    pallas_call x1, Pallas kernels, state_rows(): pl.pallas_call(rows_kernel, name='state_rows', out_shape=(shape((24, 256,...  1.43 us
  transfers between devices with their start and end apart: 4, of which 1 were waited for; matrix products, arithmetic and copies ran while one was open for 0% of the time, Pallas kernels for 16%

profile of v2, /device:TPU:24, one launch (start us, length us, event | category | flops | bytes accessed | tf_op | source)
XLA Modules:
  0.0 51.6 jit_solution(5383134478566101220)
XLA Ops:
  0.0 0.0 copy-start.2
  0.8 0.0 copy-start.5
  0.8 0.0 copy-start.6
  0.8 6.6 %observation_sums.1 = (bf16[32,80,256]{2,1,0:T(8,128)(2,1)}, bf16[1488,128]{1,0:T(8,128)(2,1)}, bf16[1488,128]{1,0:T(8,128)(2,1)}) custom-call(s32[1]{0:T(128)S(6)} %copy.16.count, s32[1]{0:T(128)} %bitcast.1.lat, bf16[64,2048]{1,0:T(8,128)(2,1)} %vals_in.1, f32[2,2048]{1,0:T(2,128)} %offs_in.1, s32[1,2048]{1,0:T(1,128)} %bitcast.7, bf16[256,24,128]{2,1,0:T(8,128)(2,1)} %state.1), custom_call_target="tpu_custom_call" | custom-call | tf_op jit(solution)/shard_map/observation_sums/pallas_call | solution.py:119
  7.4 0.0 copy-start.7
  7.5 0.1 collective-permute-start
  7.6 3.0 %collective-permute-start.1 = (bf16[1488,128]{1,0:T(8,128)(2,1)}, bf16[1488,128]{1,0:T(8,128)(2,1)S(1)}, u32[]{:S(2)}, u32[]{:S(2)}) collective-permute-start(bf16[1488,128]{1,0:T(8,128)(2,1)} %get-tuple-element.43), channel_id=1, source_target_pairs={{16,32},{48,64},{80,96},{112,128},{144,160},{176,192},{208,224},{3... | collective-permute-start | bytes 1142792 | tf_op jit(solution)/shard_map/ppermute | solution.py:438
  10.6 0.0 copy-done.2
  10.6 0.0 copy-start
  10.6 1.3 %copy-done = bf16[32,80,256]{2,1,0:T(8,128)(2,1)S(1)} copy-done((bf16[32,80,256]{2,1,0:T(8,128)(2,1)S(1)}, bf16[32,80,256]{2,1,0:T(8,128)(2,1)}, u32[]{:S(2)}) %copy-start) | copy-done | bytes 1310744
  11.9 0.0 copy-start.3
  11.9 0.0 copy-start.4
  11.9 0.0 copy-start.1
  11.9 1.4 %state_rows.1 = (bf16[24,256,128]{2,1,0:T(8,128)(2,1)S(1)}, bf16[832,128]{1,0:T(8,128)(2,1)S(1)}) custom-call(bf16[256,24,128]{2,1,0:T(8,128)(2,1)S(1)} %copy-done.2, bf16[32,80,256]{2,1,0:T(8,128)(2,1)S(1)} %copy-done), custom_call_target="tpu_custom_call" | custom-call | flops 10000000 | bytes 8000000 | tf_op jit(solution)/shard_map/state_rows/pallas_call | solution.py:168
  13.4 0.0 copy-done.5
  13.4 0.0 copy-done.6
  13.4 0.0 copy-done.7
  13.4 0.0 copy-done.3
  13.4 0.0 copy-done.4
  13.4 3.6 %prepare.1 = (bf16[128,48,224]{2,1,0:T(8,128)(2,1)S(1)}, bf16[256,80]{1,0:T(8,128)(2,1)S(1)}, bf16[1024,256]{1,0:T(8,128)(2,1)S(1)}, bf16[256,1024]{1,0:T(8,128)...) custom-call(f32[7,7,256]{2,1,0:T(8,128)S(1)} %bitcast.5, bf16[65,256]{1,0:T(8,128)(2,1)S(1)} %copy-done.6, ...), custom_call_target="tpu_custom_call" | custom-call | flops 10000000 | bytes 8000000 | tf_op jit(solution)/shard_map/prepare/pallas_call | solution.py:255
  17.0 0.0 collective-permute-done.in_a
  17.0 3.8 %collective-permute-done.1.in_b = bf16[1488,128]{1,0:T(8,128)(2,1)S(1)} collective-permute-done((bf16[1488,128]{1,0:T(8,128)(2,1)}, bf16[1488,128]{1,0:T(8,128)(2,1)S(1)}, u32[]{:S(2)}, u32[]{:S(2)}) %collective-permute-start.1) | collective-permute-done | bytes 380960 | tf_op jit(solution)/shard_map/ppermute | solution.py:438
  20.9 0.0 copy-done.1
  20.9 1.5 %edge_sums.1 = (bf16[16,80,128]{2,1,0:T(8,128)(2,1)S(1)}, bf16[416,128]{1,0:T(8,128)(2,1)S(1)}, bf16[416,128]{1,0:T(8,128)(2,1)S(1)}) custom-call(s32[1]{0:T(128)} %bitcast.1.lat, s32[1]{0:T(128)} %bitcast.lon, bf16[32,80,256]{2,1,0:T(8,128)(2,1)S(1)} %copy-done.1, bf16[832,128]{1,0:T(8,128)(2,1)S(1)} %get-tuple-element.41.rims, ...), custom_call_target="tpu_custom_call" | custom-call | tf_op jit(solution)/shard_map/edge_sums/pallas_call | solution.py:218
  22.4 0.1 collective-permute-start.2
  22.5 9.5 %collective-permute-start.3 = (bf16[416,128]{1,0:T(8,128)(2,1)S(1)}, bf16[416,128]{1,0:T(8,128)(2,1)S(1)}, u32[]{:S(2)}, u32[]{:S(2)}) collective-permute-start(bf16[416,128]{1,0:T(8,128)(2,1)S(1)} %get-tuple-element.47.out_b), channel_id=1, source_target_pairs={{1,2},{3,4},{5,6},{7,8},{9,10},{11,12},{13,14},{15,0},{2,1},{4,3},... | collective-permute-start | bytes 319496 | tf_op jit(solution)/shard_map/ppermute | solution.py:438
  31.9 0.0 copy-start.8
  32.0 0.0 copy-start.9
  32.0 0.0 copy-start.10
  32.0 0.0 copy-start.11
  32.0 0.0 copy-start.12
  32.0 3.3 %encode.1.partial = bf16[256,32,128]{2,1,0:T(8,128)(2,1)S(1)} custom-call(s32[1]{0:T(128)} %bitcast.1.lat, bf16[32,80,256]{2,1,0:T(8,128)(2,1)S(1)} %copy-done.1, bf16[16,80,128]{2,1,0:T(8,128)(2,1)S(1)} %get-tuple-element.44.edge, bf16[1488,128]{1,0:T(8,128)(2,1)S(1)} %collective-permute-done.in_a, bf16[1488,128]{1,0:T(8,128)(2,1)S(1)} %collective-permute-done.1.in_b, ...), custom_call_target="tpu_custom_call" | custom-call | flops 100000000 | bytes 8000000 | tf_op jit(solution)/shard_map/encode/pallas_call | solution.py:308
  35.3 0.0 collective-permute-done.2.in_a
  35.3 0.0 collective-permute-done.3.in_b
  35.3 0.0 copy-done.8
  35.3 0.0 copy-done.9
  35.3 0.0 copy-done.10
  35.4 0.0 copy-done.11
  35.4 0.0 copy-done.12
  35.4 16.0 %block.1 = bf16[256,24,128]{2,1,0:T(8,128)(2,1)} custom-call(s32[1]{0:T(128)} %bitcast.lon, f32[256]{0:T(256)S(1)} %copy-done.8, f32[256]{0:T(256)S(1)} %copy-done.9, f32[256]{0:T(256)S(1)} %copy-done.10, f32[256]{0:T(256)S(1)} %copy-done.11, f32[256]{0:T(256)S(1)} %copy-done.12, bf16[256,32,128]{2,1,0:T(8,128)(2,1)S(1)} %encode.1.partial, ...), custom_call_target="tpu_custom_call" | custom-call | tf_op jit(solution)/shard_map/block/pallas_call | solution.py:421
Async XLA Ops:
  0.0 10.6 %copy-start.2 = (bf16[256,24,128]{2,1,0:T(8,128)(2,1)S(1)}, bf16[256,24,128]{2,1,0:T(8,128)(2,1)}, u32[]{:S(2)}) copy-start(bf16[256,24,128]{2,1,0:T(8,128)(2,1)} %state.1) | copy-start | bytes 4718596
  0.8 12.6 %copy-start.5 = (f32[256,7,7]{0,2,1:T(8,128)S(1)}, f32[256,7,7]{0,2,1:T(8,128)}, u32[]{:S(2)}) copy-start(f32[256,7,7]{0,2,1:T(8,128)} %param.21) | copy-start | bytes 150532
  0.8 12.6 %copy-start.6 = (bf16[65,256]{1,0:T(8,128)(2,1)S(1)}, bf16[65,256]{1,0:T(8,128)(2,1)}, u32[]{:S(2)}) copy-start(bf16[65,256]{1,0:T(8,128)(2,1)} %w_in.1) | copy-start | bytes 99844
  7.4 5.9 %copy-start.7 = (f32[1024]{0:T(1024)S(1)}, f32[1024]{0:T(1024)}, u32[]{:S(2)}) copy-start(f32[1024]{0:T(1024)} %param.26) | copy-start | bytes 12292
  7.5 9.6 %collective-permute-start = (bf16[1488,128]{1,0:T(8,128)(2,1)}, bf16[1488,128]{1,0:T(8,128)(2,1)S(1)}, u32[]{:S(2)}, u32[]{:S(2)}) collective-permute-start(bf16[1488,128]{1,0:T(8,128)(2,1)} %get-tuple-element.42), channel_id=1, source_target_pairs={{0,16},{32,48},{64,80},{96,112},{128,144},{160,176},{192,208},{224... | collective-permute-start | bytes 1142792 | tf_op jit(solution)/shard_map/ppermute | solution.py:438
  7.6 13.3 %collective-permute-start.1 = (bf16[1488,128]{1,0:T(8,128)(2,1)}, bf16[1488,128]{1,0:T(8,128)(2,1)S(1)}, u32[]{:S(2)}, u32[]{:S(2)}) collective-permute-start(bf16[1488,128]{1,0:T(8,128)(2,1)} %get-tuple-element.43), channel_id=1, source_target_pairs={{16,32},{48,64},{80,96},{112,128},{144,160},{176,192},{208,224},{3... | collective-permute-start | bytes 1142792 | tf_op jit(solution)/shard_map/ppermute | solution.py:438
  10.6 1.3 %copy-start = (bf16[32,80,256]{2,1,0:T(8,128)(2,1)S(1)}, bf16[32,80,256]{2,1,0:T(8,128)(2,1)}, u32[]{:S(2)}) copy-start(bf16[32,80,256]{2,1,0:T(8,128)(2,1)} %get-tuple-element.29.sums) | copy-start | bytes 3932164
  11.9 1.5 %copy-start.3 = (bf16[256,1024]{1,0:T(8,128)(2,1)S(1)}, bf16[256,1024]{1,0:T(8,128)(2,1)}, u32[]{:S(2)}) copy-start(bf16[256,1024]{1,0:T(8,128)(2,1)} %w_up) | copy-start | bytes 1572868
  11.9 1.5 %copy-start.4 = (bf16[1024,256]{1,0:T(8,128)(2,1)S(1)}, bf16[1024,256]{1,0:T(8,128)(2,1)}, u32[]{:S(2)}) copy-start(bf16[1024,256]{1,0:T(8,128)(2,1)} %w_down) | copy-start | bytes 1572868
  11.9 8.9 %copy-start.1 = (bf16[32,80,256]{2,1,0:T(8,128)(2,1)S(1)}, bf16[32,80,256]{2,1,0:T(8,128)(2,1)}, u32[]{:S(2)}) copy-start(bf16[32,80,256]{2,1,0:T(8,128)(2,1)} %get-tuple-element.29.sums) | copy-start | bytes 3932164
  22.4 12.9 %collective-permute-start.2 = (bf16[416,128]{1,0:T(8,128)(2,1)S(1)}, bf16[416,128]{1,0:T(8,128)(2,1)S(1)}, u32[]{:S(2)}, u32[]{:S(2)}) collective-permute-start(bf16[416,128]{1,0:T(8,128)(2,1)S(1)} %get-tuple-element.46.out_a), channel_id=1, source_target_pairs={{0,1},{2,3},{4,5},{6,7},{8,9},{10,11},{12,13},{14,15},{1,0},{3,2},... | collective-permute-start | bytes 319496 | tf_op jit(solution)/shard_map/ppermute | solution.py:438
  22.5 12.8 %collective-permute-start.3 = (bf16[416,128]{1,0:T(8,128)(2,1)S(1)}, bf16[416,128]{1,0:T(8,128)(2,1)S(1)}, u32[]{:S(2)}, u32[]{:S(2)}) collective-permute-start(bf16[416,128]{1,0:T(8,128)(2,1)S(1)} %get-tuple-element.47.out_b), channel_id=1, source_target_pairs={{1,2},{3,4},{5,6},{7,8},{9,10},{11,12},{13,14},{15,0},{2,1},{4,3},... | collective-permute-start | bytes 319496 | tf_op jit(solution)/shard_map/ppermute | solution.py:438
  31.9 3.4 %copy-start.8 = (f32[256]{0:T(256)S(1)}, f32[256]{0:T(256)}, u32[]{:S(2)}) copy-start(f32[256]{0:T(256)} %dwb.1) | copy-start | bytes 3076
  32.0 3.4 %copy-start.9 = (f32[256]{0:T(256)S(1)}, f32[256]{0:T(256)}, u32[]{:S(2)}) copy-start(f32[256]{0:T(256)} %gain.1) | copy-start | bytes 3076
  32.0 3.4 %copy-start.10 = (f32[256]{0:T(256)S(1)}, f32[256]{0:T(256)}, u32[]{:S(2)}) copy-start(f32[256]{0:T(256)} %nbias.1) | copy-start | bytes 3076
  32.0 3.4 %copy-start.11 = (f32[256]{0:T(256)S(1)}, f32[256]{0:T(256)}, u32[]{:S(2)}) copy-start(f32[256]{0:T(256)} %db.1) | copy-start | bytes 3076
  32.0 3.4 %copy-start.12 = (f32[256]{0:T(256)S(1)}, f32[256]{0:T(256)}, u32[]{:S(2)}) copy-start(f32[256]{0:T(256)} %ls.1) | copy-start | bytes 3076

commit v3 on v2

--- a/solution.py
+++ b/solution.py
@@ -247,7 +247,7 @@
             toe[i * 4 + k // 2, (k % 2) * 24:(k % 2) * 24 + 24, :] = y[:, :224]
         return 0
 
-    lax.fori_loop(0, 32, step, 0)
+    lax.fori_loop(0, 32, step, 0, unroll=4)
 
 
 def prepare(dw_weight, w_in, w_up, w_down, up_bias):
@@ -293,8 +293,8 @@
         encode((8 + j, sums[8 + j, :, :128], rows[4 + j]), (16 + j, sums[16 + j, :, :128], rows[12 + j]))
         return 0
 
-    lax.fori_loop(0, 4, edge_row, 0)
-    lax.fori_loop(0, 8, inner_row, 0)
+    lax.fori_loop(0, 4, edge_row, 0, unroll=4)
+    lax.fori_loop(0, 8, inner_row, 0, unroll=4)
 
     def turn(i, _):
         c0 = pl.multiple_of(i * CB, CB)
@@ -381,7 +381,7 @@
         xbuf[:, pl.ds(c0, 16), :] = jnp.swapaxes(jnp.stack(ys, 0), 0, 1).astype(BF)
         return 0
 
-    lax.fori_loop(0, 16, norm_step, 0)
+    lax.fori_loop(0, 16, norm_step, 0, unroll=4)
 
     def mlp_step(i, _):
         x = jnp.concatenate([xbuf[i * RB + k] for k in range(RB)], 1)
@@ -407,7 +407,7 @@
 
     copies = []
     for n in range(4):
-        lax.fori_loop(4 * n, 4 * n + 4, out_step, 0)
+        lax.fori_loop(4 * n, 4 * n + 4, out_step, 0, unroll=4)
         at = slice(64 * n, 64 * n + 64)
         copies.append(pltpu.make_async_copy(result.at[at], out.at[at], sems.at[n]))
         copies[-1].start()

time: 51.6 us -> 50.1 us (0.971)
  the two profiles are of different devices: /device:TPU:24 before, /device:TPU:16 now
where the time goes in v3:
time: 50.1 us; the launch traced here: 50 us
  Pallas kernels  26.2 us (52%)
  starting transfers between devices  15.9 us (32%)
  waiting for transfers between devices  5.39 us (11%)
  local copies, waits for them, and re-layouts  1.36 us (3%)
  between operations  1.11 us (2%)
    ppermute x4, starting transfers between devices, exchange(): lax.ppermute(x, axis, pairs + [(j, i) for i, j in pairs])  15.9 us
    pallas_call x1, Pallas kernels, block(): pl.pallas_call(block_kernel, name='block', out_shape=jax.ShapeDtypeStruct...  15.6 us
    ppermute x4, waiting for transfers between devices, exchange(): lax.ppermute(x, axis, pairs + [(j, i) for i, j in pairs])  5.39 us
    pallas_call x1, Pallas kernels, observation_sums(): pl.pallas_call(sums_kernel, name='observation_sums', out_shape=(shape((RO...  3.76 us
    pallas_call x1, Pallas kernels, encode(): pl.pallas_call(encode_kernel, name='encode', in_specs=[pl.BlockSpec(memor...  1.96 us
    pallas_call x1, Pallas kernels, prepare(): pl.pallas_call(prepare_kernel, name='prepare', out_shape=(shape((128, 48,...  1.92 us
    pallas_call x1, Pallas kernels, edge_sums(): pl.pallas_call(edge_kernel, name='edge_sums', in_specs=[pl.BlockSpec(memo...  1.52 us
    pallas_call x1, Pallas kernels, state_rows(): pl.pallas_call(rows_kernel, name='state_rows', out_shape=(shape((24, 256,...  1.43 us
  transfers between devices with their start and end apart: 4, of which 2 were waited for; matrix products, arithmetic and copies ran while one was open for 0% of the time, Pallas kernels for 11%

profile of v3, /device:TPU:16, one launch (start us, length us, event | category | flops | bytes accessed | tf_op | source)
XLA Modules:
  0.0 50.0 jit_solution(8299312460636726725)
XLA Ops:
  0.0 0.0 copy-start.2
  0.8 0.0 copy-start.5
  0.8 0.0 copy-start.6
  0.8 3.8 %observation_sums.1 = (bf16[32,80,256]{2,1,0:T(8,128)(2,1)}, bf16[1488,128]{1,0:T(8,128)(2,1)}, bf16[1488,128]{1,0:T(8,128)(2,1)}) custom-call(s32[1]{0:T(128)S(6)} %copy.16.count, s32[1]{0:T(128)} %bitcast.1.lat, bf16[64,2048]{1,0:T(8,128)(2,1)} %vals_in.1, f32[2,2048]{1,0:T(2,128)} %offs_in.1, s32[1,2048]{1,0:T(1,128)} %bitcast.7, bf16[256,24,128]{2,1,0:T(8,128)(2,1)} %state.1), custom_call_target="tpu_custom_call" | custom-call | tf_op jit(solution)/shard_map/observation_sums/pallas_call | solution.py:119
  4.6 0.0 copy-start.7
  4.6 2.8 %collective-permute-start = (bf16[1488,128]{1,0:T(8,128)(2,1)}, bf16[1488,128]{1,0:T(8,128)(2,1)S(1)}, u32[]{:S(2)}, u32[]{:S(2)}) collective-permute-start(bf16[1488,128]{1,0:T(8,128)(2,1)} %get-tuple-element.42), channel_id=1, source_target_pairs={{0,16},{32,48},{64,80},{96,112},{128,144},{160,176},{192,208},{224... | collective-permute-start | bytes 1142792 | tf_op jit(solution)/shard_map/ppermute | solution.py:438
  7.4 1.9 %collective-permute-start.1 = (bf16[1488,128]{1,0:T(8,128)(2,1)}, bf16[1488,128]{1,0:T(8,128)(2,1)S(1)}, u32[]{:S(2)}, u32[]{:S(2)}) collective-permute-start(bf16[1488,128]{1,0:T(8,128)(2,1)} %get-tuple-element.43), channel_id=1, source_target_pairs={{16,32},{48,64},{80,96},{112,128},{144,160},{176,192},{208,224},{3... | collective-permute-start | bytes 1142792 | tf_op jit(solution)/shard_map/ppermute | solution.py:438
  9.3 0.0 copy-done.2
  9.3 0.0 copy-start
  9.3 1.3 %copy-done = bf16[32,80,256]{2,1,0:T(8,128)(2,1)S(1)} copy-done((bf16[32,80,256]{2,1,0:T(8,128)(2,1)S(1)}, bf16[32,80,256]{2,1,0:T(8,128)(2,1)}, u32[]{:S(2)}) %copy-start) | copy-done | bytes 1310744
  10.6 0.0 copy-start.3
  10.6 0.0 copy-start.4
  10.6 0.0 copy-start.1
  10.6 1.4 %state_rows.1 = (bf16[24,256,128]{2,1,0:T(8,128)(2,1)S(1)}, bf16[832,128]{1,0:T(8,128)(2,1)S(1)}) custom-call(bf16[256,24,128]{2,1,0:T(8,128)(2,1)S(1)} %copy-done.2, bf16[32,80,256]{2,1,0:T(8,128)(2,1)S(1)} %copy-done), custom_call_target="tpu_custom_call" | custom-call | flops 10000000 | bytes 8000000 | tf_op jit(solution)/shard_map/state_rows/pallas_call | solution.py:168
  12.1 0.0 copy-done.5
  12.1 0.0 copy-done.6
  12.1 0.0 copy-done.7
  12.1 0.0 copy-done.3
  12.1 0.0 copy-done.4
  12.1 1.9 %prepare.1 = (bf16[128,48,224]{2,1,0:T(8,128)(2,1)S(1)}, bf16[256,80]{1,0:T(8,128)(2,1)S(1)}, bf16[1024,256]{1,0:T(8,128)(2,1)S(1)}, bf16[256,1024]{1,0:T(8,128)...) custom-call(f32[7,7,256]{2,1,0:T(8,128)S(1)} %bitcast.5, bf16[65,256]{1,0:T(8,128)(2,1)S(1)} %copy-done.6, ...), custom_call_target="tpu_custom_call" | custom-call | flops 10000000 | bytes 8000000 | tf_op jit(solution)/shard_map/prepare/pallas_call | solution.py:255
  14.0 0.0 collective-permute-done.in_a
  14.1 4.4 %collective-permute-done.1.in_b = bf16[1488,128]{1,0:T(8,128)(2,1)S(1)} collective-permute-done((bf16[1488,128]{1,0:T(8,128)(2,1)}, bf16[1488,128]{1,0:T(8,128)(2,1)S(1)}, u32[]{:S(2)}, u32[]{:S(2)}) %collective-permute-start.1) | collective-permute-done | bytes 380960 | tf_op jit(solution)/shard_map/ppermute | solution.py:438
  18.5 0.0 copy-done.1
  18.5 1.5 %edge_sums.1 = (bf16[16,80,128]{2,1,0:T(8,128)(2,1)S(1)}, bf16[416,128]{1,0:T(8,128)(2,1)S(1)}, bf16[416,128]{1,0:T(8,128)(2,1)S(1)}) custom-call(s32[1]{0:T(128)} %bitcast.1.lat, s32[1]{0:T(128)} %bitcast.lon, bf16[32,80,256]{2,1,0:T(8,128)(2,1)S(1)} %copy-done.1, bf16[832,128]{1,0:T(8,128)(2,1)S(1)} %get-tuple-element.41.rims, ...), custom_call_target="tpu_custom_call" | custom-call | tf_op jit(solution)/shard_map/edge_sums/pallas_call | solution.py:218
  20.0 2.0 %collective-permute-start.2 = (bf16[416,128]{1,0:T(8,128)(2,1)S(1)}, bf16[416,128]{1,0:T(8,128)(2,1)S(1)}, u32[]{:S(2)}, u32[]{:S(2)}) collective-permute-start(bf16[416,128]{1,0:T(8,128)(2,1)S(1)} %get-tuple-element.46.out_a), channel_id=1, source_target_pairs={{0,1},{2,3},{4,5},{6,7},{8,9},{10,11},{12,13},{14,15},{1,0},{3,2},... | collective-permute-start | bytes 319496 | tf_op jit(solution)/shard_map/ppermute | solution.py:438
  22.0 9.2 %collective-permute-start.3 = (bf16[416,128]{1,0:T(8,128)(2,1)S(1)}, bf16[416,128]{1,0:T(8,128)(2,1)S(1)}, u32[]{:S(2)}, u32[]{:S(2)}) collective-permute-start(bf16[416,128]{1,0:T(8,128)(2,1)S(1)} %get-tuple-element.47.out_b), channel_id=1, source_target_pairs={{1,2},{3,4},{5,6},{7,8},{9,10},{11,12},{13,14},{15,0},{2,1},{4,3},... | collective-permute-start | bytes 319496 | tf_op jit(solution)/shard_map/ppermute | solution.py:438
  31.2 0.0 copy-start.8
  31.2 0.0 copy-start.9
  31.2 0.0 copy-start.10
  31.2 0.0 copy-start.11
  31.2 0.0 copy-start.12
  31.2 2.0 %encode.1.partial = bf16[256,32,128]{2,1,0:T(8,128)(2,1)S(1)} custom-call(s32[1]{0:T(128)} %bitcast.1.lat, bf16[32,80,256]{2,1,0:T(8,128)(2,1)S(1)} %copy-done.1, bf16[16,80,128]{2,1,0:T(8,128)(2,1)S(1)} %get-tuple-element.44.edge, bf16[1488,128]{1,0:T(8,128)(2,1)S(1)} %collective-permute-done.in_a, bf16[1488,128]{1,0:T(8,128)(2,1)S(1)} %collective-permute-done.1.in_b, ...), custom_call_target="tpu_custom_call" | custom-call | flops 100000000 | bytes 8000000 | tf_op jit(solution)/shard_map/encode/pallas_call | solution.py:308
  33.2 0.0 collective-permute-done.2.in_a
  33.2 1.0 %collective-permute-done.3.in_b = bf16[416,128]{1,0:T(8,128)(2,1)S(1)} collective-permute-done((bf16[416,128]{1,0:T(8,128)(2,1)S(1)}, bf16[416,128]{1,0:T(8,128)(2,1)S(1)}, u32[]{:S(2)}, u32[]{:S(2)}) %collective-permute-start.3) | collective-permute-done | bytes 106528 | tf_op jit(solution)/shard_map/ppermute | solution.py:438
  34.2 0.0 copy-done.8
  34.2 0.0 copy-done.9
  34.2 0.0 copy-done.10
  34.2 0.0 copy-done.11
  34.2 0.0 copy-done.12
  34.2 15.6 %block.1 = bf16[256,24,128]{2,1,0:T(8,128)(2,1)} custom-call(s32[1]{0:T(128)} %bitcast.lon, f32[256]{0:T(256)S(1)} %copy-done.8, f32[256]{0:T(256)S(1)} %copy-done.9, f32[256]{0:T(256)S(1)} %copy-done.10, f32[256]{0:T(256)S(1)} %copy-done.11, f32[256]{0:T(256)S(1)} %copy-done.12, bf16[256,32,128]{2,1,0:T(8,128)(2,1)S(1)} %encode.1.partial, ...), custom_call_target="tpu_custom_call" | custom-call | tf_op jit(solution)/shard_map/block/pallas_call | solution.py:421
Async XLA Ops:
  0.0 9.3 %copy-start.2 = (bf16[256,24,128]{2,1,0:T(8,128)(2,1)S(1)}, bf16[256,24,128]{2,1,0:T(8,128)(2,1)}, u32[]{:S(2)}) copy-start(bf16[256,24,128]{2,1,0:T(8,128)(2,1)} %state.1) | copy-start | bytes 4718596
  0.8 11.3 %copy-start.5 = (f32[256,7,7]{0,2,1:T(8,128)S(1)}, f32[256,7,7]{0,2,1:T(8,128)}, u32[]{:S(2)}) copy-start(f32[256,7,7]{0,2,1:T(8,128)} %param.21) | copy-start | bytes 150532
  0.8 11.3 %copy-start.6 = (bf16[65,256]{1,0:T(8,128)(2,1)S(1)}, bf16[65,256]{1,0:T(8,128)(2,1)}, u32[]{:S(2)}) copy-start(bf16[65,256]{1,0:T(8,128)(2,1)} %w_in.1) | copy-start | bytes 99844
  4.6 7.5 %copy-start.7 = (f32[1024]{0:T(1024)S(1)}, f32[1024]{0:T(1024)}, u32[]{:S(2)}) copy-start(f32[1024]{0:T(1024)} %param.26) | copy-start | bytes 12292
  4.6 9.5 %collective-permute-start = (bf16[1488,128]{1,0:T(8,128)(2,1)}, bf16[1488,128]{1,0:T(8,128)(2,1)S(1)}, u32[]{:S(2)}, u32[]{:S(2)}) collective-permute-start(bf16[1488,128]{1,0:T(8,128)(2,1)} %get-tuple-element.42), channel_id=1, source_target_pairs={{0,16},{32,48},{64,80},{96,112},{128,144},{160,176},{192,208},{224... | collective-permute-start | bytes 1142792 | tf_op jit(solution)/shard_map/ppermute | solution.py:438
  7.4 11.1 %collective-permute-start.1 = (bf16[1488,128]{1,0:T(8,128)(2,1)}, bf16[1488,128]{1,0:T(8,128)(2,1)S(1)}, u32[]{:S(2)}, u32[]{:S(2)}) collective-permute-start(bf16[1488,128]{1,0:T(8,128)(2,1)} %get-tuple-element.43), channel_id=1, source_target_pairs={{16,32},{48,64},{80,96},{112,128},{144,160},{176,192},{208,224},{3... | collective-permute-start | bytes 1142792 | tf_op jit(solution)/shard_map/ppermute | solution.py:438
  9.3 1.3 %copy-start = (bf16[32,80,256]{2,1,0:T(8,128)(2,1)S(1)}, bf16[32,80,256]{2,1,0:T(8,128)(2,1)}, u32[]{:S(2)}) copy-start(bf16[32,80,256]{2,1,0:T(8,128)(2,1)} %get-tuple-element.29.sums) | copy-start | bytes 3932164
  10.6 1.5 %copy-start.3 = (bf16[256,1024]{1,0:T(8,128)(2,1)S(1)}, bf16[256,1024]{1,0:T(8,128)(2,1)}, u32[]{:S(2)}) copy-start(bf16[256,1024]{1,0:T(8,128)(2,1)} %w_up) | copy-start | bytes 1572868
  10.6 1.5 %copy-start.4 = (bf16[1024,256]{1,0:T(8,128)(2,1)S(1)}, bf16[1024,256]{1,0:T(8,128)(2,1)}, u32[]{:S(2)}) copy-start(bf16[1024,256]{1,0:T(8,128)(2,1)} %w_down) | copy-start | bytes 1572868
  10.6 7.9 %copy-start.1 = (bf16[32,80,256]{2,1,0:T(8,128)(2,1)S(1)}, bf16[32,80,256]{2,1,0:T(8,128)(2,1)}, u32[]{:S(2)}) copy-start(bf16[32,80,256]{2,1,0:T(8,128)(2,1)} %get-tuple-element.29.sums) | copy-start | bytes 3932164
  20.0 13.2 %collective-permute-start.2 = (bf16[416,128]{1,0:T(8,128)(2,1)S(1)}, bf16[416,128]{1,0:T(8,128)(2,1)S(1)}, u32[]{:S(2)}, u32[]{:S(2)}) collective-permute-start(bf16[416,128]{1,0:T(8,128)(2,1)S(1)} %get-tuple-element.46.out_a), channel_id=1, source_target_pairs={{0,1},{2,3},{4,5},{6,7},{8,9},{10,11},{12,13},{14,15},{1,0},{3,2},... | collective-permute-start | bytes 319496 | tf_op jit(solution)/shard_map/ppermute | solution.py:438
  22.0 12.2 %collective-permute-start.3 = (bf16[416,128]{1,0:T(8,128)(2,1)S(1)}, bf16[416,128]{1,0:T(8,128)(2,1)S(1)}, u32[]{:S(2)}, u32[]{:S(2)}) collective-permute-start(bf16[416,128]{1,0:T(8,128)(2,1)S(1)} %get-tuple-element.47.out_b), channel_id=1, source_target_pairs={{1,2},{3,4},{5,6},{7,8},{9,10},{11,12},{13,14},{15,0},{2,1},{4,3},... | collective-permute-start | bytes 319496 | tf_op jit(solution)/shard_map/ppermute | solution.py:438
  31.2 3.0 %copy-start.8 = (f32[256]{0:T(256)S(1)}, f32[256]{0:T(256)}, u32[]{:S(2)}) copy-start(f32[256]{0:T(256)} %dwb.1) | copy-start | bytes 3076
  31.2 3.0 %copy-start.9 = (f32[256]{0:T(256)S(1)}, f32[256]{0:T(256)}, u32[]{:S(2)}) copy-start(f32[256]{0:T(256)} %gain.1) | copy-start | bytes 3076
  31.2 3.0 %copy-start.10 = (f32[256]{0:T(256)S(1)}, f32[256]{0:T(256)}, u32[]{:S(2)}) copy-start(f32[256]{0:T(256)} %nbias.1) | copy-start | bytes 3076
  31.2 3.0 %copy-start.11 = (f32[256]{0:T(256)S(1)}, f32[256]{0:T(256)}, u32[]{:S(2)}) copy-start(f32[256]{0:T(256)} %db.1) | copy-start | bytes 3076
  31.2 3.0 %copy-start.12 = (f32[256]{0:T(256)S(1)}, f32[256]{0:T(256)}, u32[]{:S(2)}) copy-start(f32[256]{0:T(256)} %ls.1) | copy-start | bytes 3076
